TPU v7x, 128 devices: a whole 4x4x4 slice. The times are simulated.
128 devices in a mesh: group: 8 (over x, core), dom: 16 (over z, y).
Axes of the slice: x: 4, y: 4, z: 4, core: 2. Of those that a mesh axis runs over, the one named last changes fastest.
Arguments:
- node_input: bfloat16 [65536, 512], P(('group', 'dom')), may hold values from -24 to 24
- virtual_input: bfloat16 [64, 512], replicated, may hold values from -24 to 24
- w_query: bfloat16 [512, 512], replicated, may hold values from -0.25 to 0.25
- w_key: bfloat16 [512, 512], replicated, may hold values from -0.25 to 0.25
- w_value: bfloat16 [512, 512], replicated, may hold values from -0.25 to 0.25
- w_out: bfloat16 [512, 512], replicated, may hold values from -0.25 to 0.25
- w_up: bfloat16 [512, 2048], replicated, may hold values from -0.25 to 0.25
- w_down: bfloat16 [2048, 512], replicated, may hold values from -0.125 to 0.125
- gain_attn: float32 [512], replicated, may hold values from 0.25 to 1.75
- gain_ffn: float32 [512], replicated, may hold values from 0.25 to 1.75
- local_nbr: int32 [65536, 8], P(('group', 'dom')), may hold values from 0 to 767, as said below
- local_len: int32 [65536], P(('group', 'dom')), may hold values from 1 to 8
- send_rows: int32 [128, 128, 16], P(('group', 'dom')), may hold values from 0 to 511
- exp_slot: int32 [65536, 4], P(('group', 'dom')), may hold values from 0 to 2047, as said below
- membership: int32 [65536], P(('group', 'dom')), may hold values from 0 to 63
Outputs:
- node_output: bfloat16 [65536, 512], P(('group', 'dom'))
- virtual_output: bfloat16 [64, 512], replicated
Inputs may be any that keep to these rules, and one draw needn't show every extreme that they name: `local_nbr`: positions 0 to 127 are the last 128 nodes of the previous shard of the same group (dom index one lower, cyclically), 128 to 639 the node's own shard, and the rest the first 128 nodes of the next shard. `exp_slot`: slot s of a receiving device is row s mod 16 of the block from device s // 16; the nodes of one device name every one of its 2048 slots exactly once.
All inputs are finite; a program needn't handle non-finite values.
Results may differ from a plain program's by a relative error of at most 0.024.
The roundings to bfloat16 on the way count: a program that leaves them out, or rounds other values in their place, can miss the bound.
Values may be sent and summed in bfloat16 or wider, within the bound.
A program may use at most 128 MiB of HBM per device.

v0:
```python
import math

import jax
import jax.numpy as jnp
from jax import lax
from jax.sharding import PartitionSpec as P

HEADS = 8
HALO = 128


def padded(block, sides, width):
    for axis, dim in sides:
        count = lax.axis_size(axis)
        forward = [(i, i + 1) for i in range(count - 1)]
        forward.append((count - 1, 0))
        backward = [(target, source) for source, target in forward]
        low = lax.ppermute(
            lax.slice_in_dim(block, block.shape[dim] - width, None, axis=dim), axis, forward
        )
        high = lax.ppermute(lax.slice_in_dim(block, 0, width, axis=dim), axis, backward)
        block = jnp.concatenate([low, block, high], axis=dim)
    return block


def layer_norm(summed, scaling):
    center = summed - jnp.mean(summed, axis=-1, keepdims=True)
    spread = jnp.mean(center * center, axis=-1, keepdims=True)
    return center * lax.rsqrt(spread + 1e-05) * scaling


def head_scores(queries, targets, head_count):
    product = queries.astype(jnp.float32) * targets.astype(jnp.float32)
    product = product.reshape(product.shape[0], head_count, -1)
    return jnp.sum(product, axis=-1) / math.sqrt(product.shape[2])


def project(inputs, weight_one):
    return jnp.dot(inputs, weight_one, preferred_element_type=jnp.float32).astype(jnp.bfloat16)


def shards(
    node_input,
    virtual_input,
    w_query,
    w_key,
    w_value,
    w_out,
    w_up,
    w_down,
    gain_attn,
    gain_ffn,
    local_nbr,
    local_len,
    send_rows,
    exp_slot,
    membership,
):
    node_rows, feat_width = node_input.shape
    head_size = feat_width // HEADS
    virt_count = virtual_input.shape[0]
    peer_count = send_rows.shape[1]
    slot_cap = send_rows.shape[2]
    w_pair = jnp.concatenate([w_key, w_value], axis=1)
    queries = project(node_input, w_query)
    key_value = project(node_input, w_pair)
    v_query = project(virtual_input, w_query)
    v_pair = project(virtual_input, w_pair)
    picks = send_rows[0].reshape(-1)
    outgoing = key_value[picks].reshape(peer_count, slot_cap, 2 * feat_width)
    arrived = lax.all_to_all(outgoing, ("group", "dom"), split_axis=0, concat_axis=0, tiled=True)
    arrived = arrived.reshape(peer_count * slot_cap, outgoing.shape[2])
    window = padded(key_value, (("dom", 0),), HALO)
    onehot = (membership[:, None] == jnp.arange(virt_count, dtype=jnp.int32)[None, :]).astype(
        jnp.bfloat16
    )
    own_pair = project(onehot, v_pair)
    local_count = local_nbr.shape[1]
    expander_count = exp_slot.shape[1]
    picked_list = [window[local_nbr[:, slot_idx]] for slot_idx in range(local_count)]
    picked_list = picked_list + [
        arrived[exp_slot[:, slot_idx]] for slot_idx in range(expander_count)
    ]
    picked_list.append(own_pair)
    scores = jnp.stack(
        [head_scores(queries, picked[:, :feat_width], HEADS) for picked in picked_list], axis=1
    )
    allowed = jnp.concatenate(
        [
            jnp.arange(local_count, dtype=jnp.int32)[None, :] < local_len[:, None],
            jnp.ones((node_rows, expander_count + 1), dtype=bool),
        ],
        axis=1,
    )
    masked = jnp.where(allowed[:, :, None], scores, -1e30)
    peak_score = jnp.max(masked, axis=1, keepdims=True)
    raised = jnp.exp(masked - peak_score)
    weights = raised / jnp.sum(raised, axis=1, keepdims=True)
    attention = jnp.zeros((node_rows, HEADS, head_size), jnp.float32)
    for slot_idx in range(len(picked_list)):
        picked_vals = picked_list[slot_idx][:, feat_width:]
        attention = attention + weights[:, slot_idx, :, None] * picked_vals.astype(
            jnp.float32
        ).reshape(node_rows, HEADS, head_size)
    attention = attention.reshape(node_rows, feat_width).astype(jnp.bfloat16)
    mixed = node_input.astype(jnp.float32) + jnp.dot(
        attention, w_out, preferred_element_type=jnp.float32
    )
    settled = layer_norm(mixed, gain_attn).astype(jnp.bfloat16)
    hidden = jnp.maximum(jnp.dot(settled, w_up, preferred_element_type=jnp.float32), 0.0).astype(
        jnp.bfloat16
    )
    node_output = layer_norm(
        settled.astype(jnp.float32) + jnp.dot(hidden, w_down, preferred_element_type=jnp.float32),
        gain_ffn,
    ).astype(jnp.bfloat16)
    vq_heads = v_query.reshape(virt_count, HEADS, head_size)
    vk_heads = v_pair[:, :feat_width].reshape(virt_count, HEADS, head_size)
    vv_heads = v_pair[:, feat_width:].astype(jnp.float32).reshape(virt_count, HEADS, head_size)
    key_heads = key_value[:, :feat_width].reshape(node_rows, HEADS, head_size)
    value_heads = key_value[:, feat_width:].astype(jnp.float32).reshape(node_rows, HEADS, head_size)
    member_scores = jnp.einsum(
        "vhc,nhc->vhn", vq_heads, key_heads, preferred_element_type=jnp.float32
    ) / math.sqrt(head_size)
    member = membership[None, None, :] == jnp.arange(virt_count, dtype=jnp.int32)[:, None, None]
    member_masked = jnp.where(member, member_scores, -1e30)
    self_score = jnp.sum(
        vq_heads.astype(jnp.float32) * vk_heads.astype(jnp.float32), axis=-1
    ) / math.sqrt(head_size)
    v_peak = jnp.maximum(lax.pmax(jnp.max(member_masked, axis=2), ("group", "dom")), self_score)
    v_raised = jnp.exp(member_masked - v_peak[:, :, None])
    part_acc = jnp.einsum(
        "vhn,nhc->vhc", v_raised, value_heads, precision=lax.Precision.HIGHEST
    ).reshape(virt_count, feat_width)
    all_total, all_acc = lax.psum((jnp.sum(v_raised, axis=2), part_acc), ("group", "dom"))
    self_raised = jnp.exp(self_score - v_peak)
    v_total = all_total + self_raised
    v_acc = all_acc.reshape(virt_count, HEADS, head_size) + self_raised[:, :, None] * vv_heads
    v_attention = (v_acc / v_total[:, :, None]).reshape(virt_count, feat_width).astype(jnp.bfloat16)
    v_mixed = virtual_input.astype(jnp.float32) + jnp.dot(
        v_attention, w_out, preferred_element_type=jnp.float32
    )
    virtual_output = layer_norm(v_mixed, gain_attn).astype(jnp.bfloat16)
    return (node_output, virtual_output)


def solution(mesh):
    placed = (
        P(("group", "dom"), None),
        P(),
        P(),
        P(),
        P(),
        P(),
        P(),
        P(),
        P(),
        P(),
        P(("group", "dom"), None),
        P(("group", "dom")),
        P(("group", "dom"), None, None),
        P(("group", "dom"), None),
        P(("group", "dom")),
    )
    return jax.shard_map(
        shards,
        mesh=mesh,
        in_specs=placed,
        out_specs=(P(("group", "dom"), None), P()),
        check_vma=False,
    )
```

profile of v0, /device:TPU:1, one launch (start us, length us, event | category | flops | bytes accessed | tf_op | source)
XLA Modules:
  0.0 437.4 jit_solution(16507267439805823532)
XLA Ops:
  14.1 9.7 %gather_fusion.8 = bf16[2048,1024]{1,0:T(8,128)(2,1)} fusion(bf16[512,1024]{1,0:T(8,128)(2,1)S(1)} %copy.156, s32[2048]{0:T(1024)S(1)} %broadcast_clamp_fusion), kind=kCustom, calls=%fused_computation.8 | custom fusion | bytes 8396800 | tf_op jit(solution)/shard_map/gather | solution.py:70
  23.8 12.0 %all-to-all-start = ((bf16[128,16,1024]{2,1,0:T(8,128)(2,1)}), bf16[128,16,1024]{2,1,0:T(8,128)(2,1)}, u32[]{:S(2)}, u32[]{:S(2)}) async-start(bf16[128,16,1024]{2,1,0:T(8,128)(2,1)} %bitcast.197), calls=%async_computation | async-start | bytes 8388608 | tf_op jit(solution)/shard_map/all_to_all | solution.py:71
  36.7 5.6 %collective-permute-start.1 = (bf16[128,1024]{0,1:T(8,128)(2,1)}, bf16[128,1024]{0,1:T(8,128)(2,1)}, u32[]{:S(2)}, u32[]{:S(2)}) collective-permute-start(bf16[128,1024]{0,1:T(8,128)(2,1)} %get-tuple-element.52), channel_id=1, source_target_pairs={{1,0},{2,1},{3,2},{4,3},{5,4},{6,5},{7,6},{8,7},{9,8},{10,9},{11,1... | collective-permute-start | bytes 786440 | tf_op jit(solution)/shard_map/ppermute | solution.py:21
  44.0 2.4 fusion.48
  46.4 99.8 %pmax.7 = f32[64,8]{0,1:T(8,128)S(1)} all-reduce(f32[64,8]{0,1:T(8,128)S(1)} %get-tuple-element.82), channel_id=1, replica_groups=mesh['group'=8,'dom'=16] {'group','dom'}, use_global_device_ids=true, to_apply=%region_20.21 | all-reduce | flops 512 | bytes 4096 | tf_op jit(solution)/shard_map/pmax | solution.py:130
  148.2 2.2 fusion.17
  156.5 64.4 %psum.15 = f32[64,8]{0,1:T(8,128)S(1)} all-reduce(f32[64,8]{0,1:T(8,128)S(1)} %fusion.16), channel_id=1, replica_groups=mesh['group'=8,'dom'=16] {'group','dom'}, use_global_device_ids=true, to_apply=%region_24.25 | all-reduce | flops 512 | bytes 4096 | tf_op jit(solution)/shard_map/psum | solution.py:135
  221.0 2.1 copy.138
  230.5 2.2 convolution_convert_fusion
  233.4 54.9 %all-reduce.3.cloned.1.call-done = f32[64,512]{1,0:T(8,128)} async-done(((f32[64,512]{1,0:T(8,128)}), f32[64,512]{1,0:T(8,128)}) %all-reduce.3.cloned.1.call-update) | async-done | bytes 131088 | tf_op jit(solution)/shard_map/psum | solution.py:135
  290.8 2.3 pad_maximum_fusion
  293.1 2.6 copy.139
  295.8 4.3 gather_fusion.7
  303.2 4.3 gather_fusion.6
  308.6 2.1 copy.200
  310.7 4.3 gather_fusion.5
  318.2 4.3 gather_fusion.4
  323.6 2.1 copy.198
  325.7 4.3 gather_fusion.3
  333.1 4.5 %gather_fusion.2 = bf16[512,1024]{1,0:T(8,128)(2,1)S(1)} fusion(bf16[768,1024]{1,0:T(8,128)(2,1)} %copy.139, s32[1024]{0:T(1024)S(1)} %get-tuple-element.95), kind=kCustom, calls=%fused_computation.2 | custom fusion | bytes 2099200 | tf_op jit(solution)/shard_map/gather | solution.py:80
  340.8 4.3 gather_fusion.1
  348.3 4.3 gather_fusion
  353.8 2.2 copy.194
  359.0 2.1 copy.185
  369.3 5.5 %gather_fusion.12 = bf16[512,1024]{1,0:T(8,128)(2,1)S(1)} fusion(bf16[2048,1024]{1,0:T(8,128)(2,1)} %bitcast.27, s32[1024]{0:T(1024)S(1)} %get-tuple-element.86), kind=kCustom, calls=%fused_computation.12 | custom fusion | bytes 2099200 | tf_op jit(solution)/shard_map/gather | solution.py:82
  375.8 2.1 copy.205
  377.9 5.5 %gather_fusion.11 = bf16[512,1024]{1,0:T(8,128)(2,1)S(1)} fusion(bf16[2048,1024]{1,0:T(8,128)(2,1)} %bitcast.27, s32[1024]{0:T(1024)S(1)} %get-tuple-element.87), kind=kCustom, calls=%fused_computation.11 | custom fusion | bytes 2099200 | tf_op jit(solution)/shard_map/gather | solution.py:82
  386.5 5.7 %gather_fusion.10 = bf16[512,1024]{1,0:T(8,128)(2,1)S(1)} fusion(bf16[2048,1024]{1,0:T(8,128)(2,1)} %bitcast.27, s32[1024]{0:T(1024)S(1)} %get-tuple-element.88), kind=kCustom, calls=%fused_computation.10 | custom fusion | bytes 2099200 | tf_op jit(solution)/shard_map/gather | solution.py:82
  395.4 5.5 %gather_fusion.9 = bf16[512,1024]{1,0:T(8,128)(2,1)S(1)} fusion(bf16[2048,1024]{1,0:T(8,128)(2,1)} %bitcast.27, s32[1024]{0:T(1024)S(1)} %get-tuple-element.89), kind=kCustom, calls=%fused_computation.9 | custom fusion | bytes 2099200 | tf_op jit(solution)/shard_map/gather | solution.py:82
  404.0 2.2 copy.190
  412.4 5.4 %bitcast_reduce_fusion = (f32[512,8]{0,1:T(8,128)S(1)}, f32[512,8]{0,1:T(8,128)S(1)}, f32[512,8]{0,1:T(8,128)S(1)}, f32[512,8]{0,1:T(8,128)S(1)}, f32[512,8]{0,1...) fusion(bf16[512,1024]{0,1:T(8,128)(2,1)S(1)} %copy-done.2, ...), kind=kOutput, calls=%fused_computation.66 | convolution fusion | flops 279130112 | bytes 8077312 | tf_op jit(solution)/shard_map/dot_general | solution.py:39
  421.3 5.1 %fusion.47 = (f32[512]{0:T(512)S(1)}, f32[512,512]{0,1:T(8,128)}) fusion(bf16[2048,512]{1,0:T(8,128)(2,1)S(1)} %copy-done, bf16[512,2048]{1,0:T(8,128)(2,1)} %param.21, f32[512,512]{0,1:T(8,128)S(1)} %get-tuple-element.79, f32[512]{0:T(512)S(1)} %copy-done.27, f32[512]{0:T(512)S(1)} %add_rsqrt_fusion.1, f32[512]{0:T(512)S(1)} %broadcast_multiply_fusion.1), kind=kOutput, calls=%fused_computation.184 | convolution fusion | flops 2152463872 | bytes 6299648 | tf_op jit(solution)/shard_map/dot_general | solution.py:114
  (164 shorter events, 81.8 us)
Async XLA Ops:
  7.2 414.1 %copy-start = (bf16[2048,512]{1,0:T(8,128)(2,1)S(1)}, bf16[2048,512]{1,0:T(8,128)(2,1)}, u32[]{:S(2)}) copy-start(bf16[2048,512]{1,0:T(8,128)(2,1)} %param.22) | copy-start | bytes 6291460
  7.2 3.5 copy-start.24
  9.6 1.1 copy-start.3
  10.7 3.2 copy-start.26
  23.8 12.0 %copy-start.1 = (bf16[512,1024]{0,1:T(8,128)(2,1)S(1)}, bf16[512,1024]{0,1:T(8,128)(2,1)}, u32[]{:S(2)}) copy-start(bf16[512,1024]{0,1:T(8,128)(2,1)} %fusion.2) | copy-start | bytes 3145732
  23.8 345.5 %all-to-all-start = ((bf16[128,16,1024]{2,1,0:T(8,128)(2,1)}), bf16[128,16,1024]{2,1,0:T(8,128)(2,1)}, u32[]{:S(2)}, u32[]{:S(2)}) async-start(bf16[128,16,1024]{2,1,0:T(8,128)(2,1)} %bitcast.197), calls=%async_computation | async-start | bytes 8388608 | tf_op jit(solution)/shard_map/all_to_all | solution.py:71
  35.8 7.5 %copy-start.22 = (bf16[64,512]{1,0:T(8,128)(2,1)S(1)}, bf16[64,512]{1,0:T(8,128)(2,1)}, u32[]{:S(2)}) copy-start(bf16[64,512]{1,0:T(8,128)(2,1)} %param.16) | copy-start | bytes 196612
  35.8 252.6 %all-reduce.3.cloned.1.call-start = ((), (), s32[]{:S(2)}) async-start(), calls=%async_computation.1 | async-start | bytes 262144 | tf_op jit(solution)/shard_map/psum | solution.py:135
  35.8 7.5 %copy-start.4 = (bf16[512,1024]{1,0:T(8,128)(2,1)S(1)}, bf16[512,1024]{1,0:T(8,128)(2,1)}, u32[]{:S(2)}) copy-start(bf16[512,1024]{1,0:T(8,128)(2,1)} %copy-done.3) | copy-start | bytes 3145732
  35.8 7.8 %copy-start.23 = (bf16[512,512]{1,0:T(8,128)(2,1)S(1)}, bf16[512,512]{1,0:T(8,128)(2,1)}, u32[]{:S(2)}) copy-start(bf16[512,512]{1,0:T(8,128)(2,1)} %param.17) | copy-start | bytes 1572868
  36.7 254.1 %collective-permute-start.1 = (bf16[128,1024]{0,1:T(8,128)(2,1)}, bf16[128,1024]{0,1:T(8,128)(2,1)}, u32[]{:S(2)}, u32[]{:S(2)}) collective-permute-start(bf16[128,1024]{0,1:T(8,128)(2,1)} %get-tuple-element.52), channel_id=1, source_target_pairs={{1,0},{2,1},{3,2},{4,3},{5,4},{6,5},{7,6},{8,7},{9,8},{10,9},{11,1... | collective-permute-start | bytes 786440 | tf_op jit(solution)/shard_map/ppermute | solution.py:21
  42.2 1.7 copy-start.25
  42.2 248.5 %collective-permute-start = (bf16[128,1024]{0,1:T(8,128)(2,1)}, bf16[128,1024]{0,1:T(8,128)(2,1)}, u32[]{:S(2)}, u32[]{:S(2)}) collective-permute-start(bf16[128,1024]{0,1:T(8,128)(2,1)} %get-tuple-element.51), channel_id=1, source_target_pairs={{0,1},{1,2},{2,3},{3,4},{4,5},{5,6},{6,7},{7,8},{8,9},{9,10},{10,1... | collective-permute-start | bytes 786440 | tf_op jit(solution)/shard_map/ppermute | solution.py:18
  226.1 64.0 %copy-start.27 = (f32[512]{0:T(512)S(1)}, f32[512]{0:T(512)}, u32[]{:S(2)}) copy-start(f32[512]{0:T(512)} %param.23) | copy-start | bytes 6148
  353.8 4.2 copy-start.21
  358.0 7.2 %copy-start.20 = (bf16[512,512]{1,0:T(8,128)(2,1)S(1)}, bf16[512,512]{1,0:T(8,128)(2,1)}, u32[]{:S(2)}) copy-start(bf16[512,512]{1,0:T(8,128)(2,1)} %get-tuple-element.39) | copy-start | bytes 1572868
  359.0 7.3 %copy-start.19 = (bf16[512,512]{1,0:T(8,128)(2,1)S(1)}, bf16[512,512]{1,0:T(8,128)(2,1)}, u32[]{:S(2)}) copy-start(bf16[512,512]{1,0:T(8,128)(2,1)} %get-tuple-element.37) | copy-start | bytes 1572868
  404.0 8.4 %copy-start.2 = (bf16[512,1024]{0,1:T(8,128)(2,1)S(1)}, bf16[512,1024]{0,1:T(8,128)(2,1)}, u32[]{:S(2)}) copy-start(bf16[512,1024]{0,1:T(8,128)(2,1)} %convolution_convert_fusion) | copy-start | bytes 3145732
  412.3 5.9 %copy-start.8 = (bf16[512,512]{0,1:T(8,128)(2,1)S(1)}, bf16[512,512]{0,1:T(8,128)(2,1)}, u32[]{:S(2)}) copy-start(bf16[512,512]{0,1:T(8,128)(2,1)} %copy.198) | copy-start | bytes 1572868
  412.3 5.9 %copy-start.9 = (bf16[512,512]{0,1:T(8,128)(2,1)S(1)}, bf16[512,512]{0,1:T(8,128)(2,1)}, u32[]{:S(2)}) copy-start(bf16[512,512]{0,1:T(8,128)(2,1)} %copy.197) | copy-start | bytes 1572868
  412.3 5.9 %copy-start.10 = (bf16[512,512]{0,1:T(8,128)(2,1)S(1)}, bf16[512,512]{0,1:T(8,128)(2,1)}, u32[]{:S(2)}) copy-start(bf16[512,512]{0,1:T(8,128)(2,1)} %copy.196) | copy-start | bytes 1572868
  412.4 5.9 %copy-start.11 = (bf16[512,512]{0,1:T(8,128)(2,1)S(1)}, bf16[512,512]{0,1:T(8,128)(2,1)}, u32[]{:S(2)}) copy-start(bf16[512,512]{0,1:T(8,128)(2,1)} %copy.195) | copy-start | bytes 1572868
  412.4 5.9 %copy-start.12 = (bf16[512,512]{0,1:T(8,128)(2,1)S(1)}, bf16[512,512]{0,1:T(8,128)(2,1)}, u32[]{:S(2)}) copy-start(bf16[512,512]{0,1:T(8,128)(2,1)} %copy.194) | copy-start | bytes 1572868
  412.4 5.9 %copy-start.13 = (bf16[512,512]{0,1:T(8,128)(2,1)S(1)}, bf16[512,512]{0,1:T(8,128)(2,1)}, u32[]{:S(2)}) copy-start(bf16[512,512]{0,1:T(8,128)(2,1)} %copy.205) | copy-start | bytes 1572868
  412.4 5.9 %copy-start.14 = (bf16[512,512]{0,1:T(8,128)(2,1)S(1)}, bf16[512,512]{0,1:T(8,128)(2,1)}, u32[]{:S(2)}) copy-start(bf16[512,512]{0,1:T(8,128)(2,1)} %copy.204) | copy-start | bytes 1572868
  412.4 5.9 %copy-start.15 = (bf16[512,512]{0,1:T(8,128)(2,1)S(1)}, bf16[512,512]{0,1:T(8,128)(2,1)}, u32[]{:S(2)}) copy-start(bf16[512,512]{0,1:T(8,128)(2,1)} %copy.203) | copy-start | bytes 1572868
  412.4 5.9 %copy-start.16 = (bf16[512,512]{0,1:T(8,128)(2,1)S(1)}, bf16[512,512]{0,1:T(8,128)(2,1)}, u32[]{:S(2)}) copy-start(bf16[512,512]{0,1:T(8,128)(2,1)} %copy.202) | copy-start | bytes 1572868
  417.8 1.2 copy-start.6
  417.9 1.3 copy-start.7
  419.2 1.3 copy-start.17
  419.2 1.3 copy-start.18
  421.2 6.5 %copy-start.28 = (f32[512]{0:T(512)S(1)}, f32[512]{0:T(512)}, u32[]{:S(2)}) copy-start(f32[512]{0:T(512)} %param.24) | copy-start | bytes 6148
  (1 other events, 1.0 us)
Sparse Core Ops, SparseCore 0:
  151.3 137.0 all-reduce.2
where the time goes:
time: 445 us; the launch traced here: 437 us
  blocking collectives  164 us (37%)
  local copies, waits for them, and re-layouts  146 us (33%)
  waiting for transfers between devices  55 us (12%)
  matrix products  21.5 us (5%)
  other arithmetic  17.7 us (4%)
  starting transfers between devices  17.6 us (4%)
  between operations  15.2 us (3%)
    pmax x1, blocking collectives, shards(): lax.pmax(jnp.max(member_masked, axis=2), ('group', 'dom'))  99.8 us
    psum x1, blocking collectives, shards(): lax.psum((jnp.sum(v_raised, axis=2), part_acc), ('group', 'dom'))  64.4 us
    psum x1, waiting for transfers between devices, shards(): lax.psum((jnp.sum(v_raised, axis=2), part_acc), ('group', 'dom'))  54.9 us
    unnamed x86, local copies, waits for them, and re-layouts  53.1 us
    gather x8, local copies, waits for them, and re-layouts, shards(): window[local_nbr[:, slot_idx]]  34.9 us
    gather x4, local copies, waits for them, and re-layouts, shards(): arrived[exp_slot[:, slot_idx]]  22.1 us
    slice x12, local copies, waits for them, and re-layouts, shards(): picked[:, :feat_width]  12.9 us
    all_to_all x1, starting transfers between devices, shards(): lax.all_to_all(outgoing, ('group', 'dom'), split_axis=0, concat_axis=0, t...  12 us
  transfers between devices with their start and end apart: 4, of which 1 were waited for; matrix products, arithmetic and copies ran while one was open for 25% of the time, Pallas kernels for 0%

commit v1 on v0

v1 whole, which is shorter than its diff:
```python
import functools

import jax
import jax.numpy as jnp
from jax import lax
from jax.experimental import pallas as pl
from jax.experimental.pallas import tpu as pltpu
from jax.sharding import PartitionSpec as P

MESH = pl.DeviceIdType.MESH
BF = jnp.bfloat16
F32 = jnp.float32
NEG = -1e30

D = 512
H = 8
HD = D // H
N = 512
VN = 64
HALO = 128
CAP = 16
BLK = 256
OWN_BLOCKS = N // BLK
FIRST_EXP = OWN_BLOCKS + 1
GROUPS = 8
BLOCKS = FIRST_EXP + GROUPS
ROWS = BLOCKS * BLK
EXP0 = FIRST_EXP * BLK
PART = D + 256


def dot(a, b, dims=((1,), (0,)), precision=None):
    return lax.dot_general(a, b, (dims, ((), ())), precision=precision, preferred_element_type=F32)


NT = ((1,), (1,))


def iota(shape, dim):
    return lax.broadcasted_iota(jnp.int32, shape, dim)


def norm(u, gain):
    center = u - jnp.mean(u, axis=-1, keepdims=True)
    spread = jnp.mean(center * center, axis=-1, keepdims=True)
    return center * lax.rsqrt(spread + 1e-05) * gain


def expander(rows):
    return (iota((rows, D), 1) // HD == iota((rows, D), 0)).astype(F32)


def wrap(value, size):
    return jnp.where(value >= size, value - size, value)


def kernel(
    x_hbm, vx_hbm, wq_hbm, wk_hbm, wv_hbm, wo_hbm, wu_hbm, wd_hbm, ga_hbm, gf_hbm,
    nbr_hbm, len_hbm, rows_hbm, slot_hbm, mem_hbm,
    out_hbm, vout_hbm,
    xall, vx, wq, wk, wv, wo, wu, wd, ga, gf, nbr, length, rows, slot, mem,
    send, wvt, qm, bias, kblk, vt, m_ref, l_ref, acc, att, outs,
    vq32, vk32, vv32, vkey, vbias, part, r1, c1, r2, r3a, r3, vrow, vout,
    in_sem, out_sem, ssem, rsem, halo_s, halo_r, s1s, s1r, s2s, s2r, s3s, s3r, s4s, s4r,
):
    g = lax.axis_index("group")
    d = lax.axis_index("dom")
    x, c = g // 2, g % 2
    z, y = d // 4, d % 4

    order = [
        (x_hbm, xall.at[pl.ds(0, N)]), (rows_hbm, rows), (wq_hbm, wq), (wk_hbm, wk), (wv_hbm, wv),
        (vx_hbm, vx), (mem_hbm, mem), (len_hbm, length), (nbr_hbm, nbr), (slot_hbm, slot),
        (ga_hbm, ga), (gf_hbm, gf), (wo_hbm, wo), (wu_hbm, wu), (wd_hbm, wd),
    ]
    loads = [pltpu.make_async_copy(a, b, in_sem.at[i]) for i, (a, b) in enumerate(order)]
    for load in loads:
        load.start()

    barrier = pltpu.get_barrier_semaphore()
    others = [wrap(g + i, H) for i in range(8)]

    def greet(dom, first):
        for i in range(first, 8):
            pl.semaphore_signal(barrier, inc=1, device_id=(others[i], dom), device_id_type=MESH)

    greet(d, 1)

    def greet_dom(i, carry):
        greet(wrap(d + i, 16), 0)
        return carry

    lax.fori_loop(1, 16, greet_dom, 0)

    loads[0].wait()
    loads[1].wait()
    picks = rows[...]
    lanes16 = iota((CAP, N), 1)
    for chunk in range(8):
        hot = jnp.concatenate(
            [
                (picks[:, chunk * 16 + i : chunk * 16 + i + 1] == lanes16).astype(F32).astype(BF)
                for i in range(16)
            ],
            axis=0,
        )
        send[pl.ds(chunk * 256, 256), :] = dot(hot, xall[pl.ds(0, N), :]).astype(BF)

    pl.semaphore_wait(barrier, 127)

    up, down = wrap(d + 1, 16), wrap(d + 15, 16)
    to_up = pltpu.make_async_remote_copy(
        xall.at[pl.ds(N - HALO, HALO)], xall.at[pl.ds(N + HALO, HALO)],
        halo_s.at[0], halo_r.at[0], device_id=(g, up), device_id_type=MESH,
    )
    to_down = pltpu.make_async_remote_copy(
        xall.at[pl.ds(0, HALO)], xall.at[pl.ds(N, HALO)],
        halo_s.at[1], halo_r.at[1], device_id=(g, down), device_id_type=MESH,
    )
    to_up.start()
    to_down.start()

    ty = [wrap(y + i, 4) for i in range(4)]
    tc = [c, 1 - c]

    def post(group, kz, first):
        kc, jx = group % 2, group // 2
        tz = wrap(z + kz, 4)
        xb = wrap(x + kz, 4)
        for ky in range(first, 4):
            tg = wrap(xb + (jx + ky) % 4, 4) * 2 + tc[kc]
            td = tz * 4 + ty[ky]
            pltpu.make_async_remote_copy(
                send.at[pl.ds(pl.multiple_of((tg * 16 + td) * CAP, CAP), CAP)],
                xall.at[pl.ds(pl.multiple_of(EXP0 + group * BLK + (kz * 4 + ky) * CAP, CAP), CAP)],
                ssem, rsem.at[group], device_id=(tg, td), device_id_type=MESH,
            ).start()

    for group in range(GROUPS):
        if group == 0:
            post(0, 0, 1)

        def post_z(kz, carry):
            post(group, kz, 0)
            return carry

        lax.fori_loop(1 if group == 0 else 0, 4, post_z, 0)
    me = g * 16 + d
    xall[pl.ds(EXP0, CAP), :] = send[pl.ds(pl.multiple_of(me * CAP, CAP), CAP), :]

    for i in range(2, 12):
        loads[i].wait()
    half = iota((BLK, 128), 1) // HD
    for r in range(0, N, BLK):
        q = (dot(xall[pl.ds(r, BLK), :], wq[...]).astype(BF) * 0.125).astype(F32)
        for h in range(H):
            pair = q[:, h // 2 * 128 : h // 2 * 128 + 128]
            qm[h, pl.ds(r, BLK), :] = jnp.where(half == h % 2, pair, 0.0).astype(BF)
    wvt[...] = wv[...].T
    vq32[...] = dot(vx[...], wq[...]).astype(BF).astype(F32) * 0.125
    vkey[...] = dot(vx[...], wk[...]).astype(BF)
    vk32[...] = vkey[...].astype(F32)
    vval = dot(vx[...], wv[...]).astype(BF)
    vv32[...] = vval.astype(F32)

    member_row = mem[...]
    member = iota((VN, N), 0) == member_row
    k_own = dot(xall[pl.ds(0, N), :], wk[...]).astype(BF)
    v_own = dot(xall[pl.ds(0, N), :], wv[...]).astype(BF)
    head_of = iota((VN, D), 1) // HD
    lane = iota((VN, 128), 1)
    part_acc = jnp.zeros((VN, D), F32)
    part_max = jnp.zeros((VN, 128), F32)
    part_sum = jnp.zeros((VN, 128), F32)
    for h in range(H):
        pair = slice(h // 2 * 128, h // 2 * 128 + 128)
        vqh = jnp.where(head_of == h, vq32[...], 0.0).astype(BF)[:, pair]
        s = jnp.where(member, dot(vqh, k_own[:, pair], NT), NEG)
        top = jnp.max(s, axis=1, keepdims=True)
        p = jnp.where(member, jnp.exp(s - top), 0.0)
        part_max = jnp.where(lane == h, top, part_max)
        part_sum = jnp.where(lane == h, jnp.sum(p, axis=1, keepdims=True), part_sum)
        high = p.astype(BF)
        low = (p - high.astype(F32)).astype(BF)
        o = dot(high, v_own) + dot(low, v_own)
        part_acc = jnp.where(head_of == h, o, part_acc)
    part[:, pl.ds(0, D)] = part_acc
    part[:, pl.ds(D, 128)] = part_max
    part[:, pl.ds(D + 128, 128)] = part_sum
    for i in range(1, 8):
        pltpu.make_async_remote_copy(
            part.at[pl.ds(pl.multiple_of(others[i] * 8, 8), 8)], r1.at[g],
            s1s, s1r, device_id=(others[i], d), device_id_type=MESH,
        ).start()
    r1[g] = part[pl.ds(pl.multiple_of(g * 8, 8), 8), :]

    win = nbr[...] - HALO
    win = jnp.where(win < 0, win + EXP0, win)
    win = jnp.where(iota((8, N), 0) < length[...], win, -1)
    for r in range(0, EXP0, 64):
        row = iota((64, N), 0) + r
        count = jnp.zeros((64, N), F32)
        for e in range(8):
            count = count + jnp.where(win[e : e + 1, :] == row, 1.0, 0.0)
        bias[pl.ds(r, 64), :] = jnp.where(count > 0.0, jnp.log(jnp.maximum(count, 1.0)), NEG)
    source = slot[...] // CAP
    sg, sd = source // 16, source % 16
    kz = (z - sd // 4 + 4) % 4
    ky = (y - sd % 4 + 4) % 4
    kc = (c - sg % 2 + 2) % 2
    kx = (x - sg // 2 + 4) % 4
    jx = (kx - kz - ky + 8) % 4
    spot = (jx * 2 + kc) * BLK + (kz * 4 + ky) * CAP + slot[...] % CAP

    def expander_bias(i, carry):
        r = pl.multiple_of(i * 64, 64)
        row = iota((64, N), 0) + r
        hit = spot[0:1, :] == row
        for e in range(1, 4):
            hit = hit | (spot[e : e + 1, :] == row)
        bias[pl.ds(EXP0 + r, 64), :] = jnp.where(hit, 0.0, NEG)
        return carry

    lax.fori_loop(0, GROUPS * BLK // 64, expander_bias, 0)

    vvt = vval.T
    vbias[...] = jnp.where(member, 0.0, NEG)
    for h in range(H):
        pair = slice(h // 2 * 128, h // 2 * 128 + 128)
        s = dot(vkey[:, pair], qm[h], NT) + vbias[...]
        top = jnp.max(s, axis=0, keepdims=True)
        p = jnp.exp(s - top)
        m_ref[h : h + 1, :] = top
        l_ref[h : h + 1, :] = jnp.sum(p, axis=0, keepdims=True)
        acc[h * HD : (h + 1) * HD, :] = dot(vvt[h * HD : (h + 1) * HD, :], p.astype(BF))

    def wait_bytes(like, sem):
        pltpu.make_async_copy(like, like, sem).wait()

    expand = expander(128)

    def combine(parts):
        tops = [q[:, D : D + 128] for q in parts]
        top = functools.reduce(jnp.maximum, tops)
        scale = [jnp.exp(t - top) for t in tops]
        total = functools.reduce(jnp.add, [q[:, D + 128 :] * f for q, f in zip(parts, scale)])
        wide = dot(jnp.concatenate(scale, axis=0), expand, precision=lax.Precision.HIGHEST)
        n = parts[0].shape[0]
        mixed = functools.reduce(
            jnp.add, [q[:, :D] * wide[i * n : (i + 1) * n, :] for i, q in enumerate(parts)]
        )
        return mixed, top, total

    def block(b, carry):
        @pl.when(b == OWN_BLOCKS)
        def _():
            to_up.wait_recv()
            to_down.wait_recv()

        @pl.when(b == FIRST_EXP)
        def _():
            wait_bytes(xall.at[pl.ds(EXP0, 15 * CAP)], rsem.at[0])

        @pl.when(b > FIRST_EXP)
        def _():
            wait_bytes(xall.at[pl.ds(EXP0, 16 * CAP)], rsem.at[b - FIRST_EXP])

        @pl.when(b == FIRST_EXP)
        def _():
            wait_bytes(r1.at[pl.ds(0, 7)], s1r)
            mixed, top, total = combine([r1[i] for i in range(8)])
            for i in range(8):
                c1[i, :, pl.ds(0, D)] = mixed[i : i + 1, :]
                c1[i, :, pl.ds(D, 128)] = top[i : i + 1, :]
                c1[i, :, pl.ds(D + 128, 128)] = total[i : i + 1, :]

            for i in range(8):
                @pl.when(d != i)
                def _():
                    pltpu.make_async_remote_copy(
                        c1.at[i], r2.at[d], s2s, s2r, device_id=(g, i), device_id_type=MESH
                    ).start()

            @pl.when(d < 8)
            def _():
                r2[d] = c1[d]

        @pl.when((b == FIRST_EXP + 2) & (d < 8))
        def _():
            wait_bytes(r2.at[pl.ds(0, 15)], s2r)
            mixed, top, total = combine([r2[i] for i in range(16)])
            v = g * 8 + d
            vq, vk, vv = vq32[pl.ds(v, 1), :], vk32[pl.ds(v, 1), :], vv32[pl.ds(v, 1), :]
            eight = lambda row: jnp.broadcast_to(row, (8, row.shape[1]))
            own = dot(eight(vq * vk), expand, NT, precision=lax.Precision.HIGHEST)[0:1, :]
            peak = jnp.maximum(top, own)
            old, new = jnp.exp(top - peak), jnp.exp(own - peak)
            denom = total * old + new
            factors = jnp.concatenate([old, new, denom], axis=0)
            factors = jnp.concatenate([factors, jnp.zeros((5, 128), F32)], axis=0)
            wide = dot(factors, expand, precision=lax.Precision.HIGHEST)
            va = (mixed * wide[0:1, :] + wide[1:2, :] * vv) / wide[2:3, :]
            proj = dot(eight(va).astype(BF), wo[...])
            u = eight(vx_row(v)) + proj
            vrow[0] = norm(u, ga[...]).astype(BF).astype(F32)[0:1, :]
            for i in range(1, 16):
                pltpu.make_async_remote_copy(
                    vrow.at[0], r3a.at[d], s3s, s3r,
                    device_id=(g, wrap(d + i, 16)), device_id_type=MESH,
                ).start()
            r3a[d] = vrow[0]

        @pl.when(b == FIRST_EXP + 5)
        def _():
            @pl.when(d < 8)
            def _():
                wait_bytes(r3a.at[pl.ds(0, 7)], s3r)

            @pl.when(d >= 8)
            def _():
                wait_bytes(r3a.at[pl.ds(0, 8)], s3r)

            r3[g] = r3a[:, 0, :]
            for i in range(1, 8):
                pltpu.make_async_remote_copy(
                    r3.at[g], r3.at[g], s4s, s4r, device_id=(others[i], d), device_id_type=MESH
                ).start()

        r = pl.multiple_of(b * BLK, BLK)
        xb = xall[pl.ds(r, BLK), :]
        kblk[...] = dot(xb, wk[...]).astype(BF)
        vt[...] = dot(wvt[...], xb, NT).astype(BF)
        for h in range(H):
            pair = slice(h // 2 * 128, h // 2 * 128 + 128)
            s = dot(kblk[:, pair], qm[h], NT) + bias[pl.ds(r, BLK), :]
            old = m_ref[h : h + 1, :]
            top = jnp.maximum(old, jnp.max(s, axis=0, keepdims=True))
            keep = jnp.exp(old - top)
            p = jnp.exp(s - top)
            m_ref[h : h + 1, :] = top
            l_ref[h : h + 1, :] = l_ref[h : h + 1, :] * keep + jnp.sum(p, axis=0, keepdims=True)
            span = slice(h * HD, (h + 1) * HD)
            acc[span, :] = acc[span, :] * keep + dot(vt[span, :], p.astype(BF))
        return carry

    def vx_row(v):
        return vx32_row(vx, v)

    loads[12].wait()
    lax.fori_loop(0, BLOCKS, block, 0)

    for h in range(H):
        span = slice(h * HD, (h + 1) * HD)
        att[span, :] = (acc[span, :] * (1.0 / l_ref[h : h + 1, :])).astype(BF)
    loads[13].wait()
    loads[14].wait()
    attn = att[...].T
    att[...] = attn
    for r in range(0, N, BLK):
        at = pl.ds(r, BLK)
        mixed = xall[at, :].astype(F32) + dot(att[at, :], wo[...])
        settled = norm(mixed, ga[...]).astype(BF)
        total = settled.astype(F32)
        for f in range(0, 4 * D, D):
            hidden = jnp.maximum(dot(settled, wu[:, f : f + D]), 0.0).astype(BF)
            total = total + dot(hidden, wd[f : f + D, :])
        outs[at, :] = norm(total, gf[...]).astype(BF)
        pltpu.make_async_copy(outs.at[at], out_hbm.at[at], out_sem.at[r // BLK]).start()

    wait_bytes(r3.at[pl.ds(0, 7)], s4r)
    vout[...] = r3[...].reshape(VN, D).astype(BF)
    last = pltpu.make_async_copy(vout, vout_hbm, out_sem.at[2])
    last.start()

    to_up.wait_send()
    to_down.wait_send()
    wait_bytes(send.at[pl.ds(0, 127 * CAP)], ssem)
    wait_bytes(part.at[pl.ds(0, 56)], s1s)

    @pl.when(d < 8)
    def _():
        wait_bytes(c1.at[pl.ds(0, 7)], s2s)
        wait_bytes(r2.at[pl.ds(0, 15), :, pl.ds(0, D)], s3s)

    @pl.when(d >= 8)
    def _():
        wait_bytes(c1, s2s)

    wait_bytes(r3.at[pl.ds(0, 7)], s4s)
    for r in range(0, N, BLK):
        at = pl.ds(r, BLK)
        pltpu.make_async_copy(outs.at[at], out_hbm.at[at], out_sem.at[r // BLK]).wait()
    last.wait()


def vx32_row(vx, v):
    hot = (iota((8, VN), 1) == v).astype(F32).astype(BF)
    return dot(hot, vx[...])[0:1, :]


def shards(
    node_input, virtual_input, w_query, w_key, w_value, w_out, w_up, w_down, gain_attn, gain_ffn,
    local_nbr, local_len, send_rows, exp_slot, membership,
):
    args = (
        node_input, virtual_input, w_query, w_key, w_value, w_out, w_up, w_down,
        gain_attn.reshape(1, D), gain_ffn.reshape(1, D), local_nbr.T, local_len.reshape(1, N),
        send_rows[0].T, exp_slot.T, membership.reshape(1, N),
    )
    vmem = pltpu.VMEM
    dma = pltpu.SemaphoreType.DMA
    scratch = [
        vmem((ROWS, D), BF), vmem((VN, D), BF), vmem((D, D), BF), vmem((D, D), BF),
        vmem((D, D), BF), vmem((D, D), BF), vmem((D, 4 * D), BF), vmem((4 * D, D), BF),
        vmem((1, D), F32), vmem((1, D), F32), vmem((8, N), jnp.int32), vmem((1, N), jnp.int32),
        vmem((CAP, 128), jnp.int32), vmem((4, N), jnp.int32), vmem((1, N), jnp.int32),
        vmem((128 * CAP, D), BF), vmem((D, D), BF), vmem((H, N, 128), BF), vmem((ROWS, N), F32),
        vmem((BLK, D), BF), vmem((D, BLK), BF), vmem((H, N), F32), vmem((H, N), F32),
        vmem((D, N), F32), vmem((D, N), BF), vmem((N, D), BF),
        vmem((VN, D), F32), vmem((VN, D), F32), vmem((VN, D), F32), vmem((VN, D), BF),
        vmem((VN, N), F32), vmem((VN, PART), F32), vmem((8, 8, PART), F32),
        vmem((8, 1, PART), F32), vmem((16, 1, PART), F32), vmem((8, 1, D), F32),
        vmem((8, 8, D), F32), vmem((1, 1, D), F32), vmem((VN, D), BF),
        dma((15,)), dma((3,)), dma, dma((GROUPS,)), dma((2,)), dma((2,)),
        dma, dma, dma, dma, dma, dma, dma, dma,
    ]
    hbm = pl.BlockSpec(memory_space=pl.ANY)
    return pl.pallas_call(
        kernel,
        out_shape=(
            jax.ShapeDtypeStruct((N, D), BF),
            jax.ShapeDtypeStruct((VN, D), BF),
        ),
        in_specs=[hbm] * len(args),
        out_specs=(hbm, hbm),
        scratch_shapes=scratch,
        compiler_params=pltpu.CompilerParams(
            collective_id=0, has_side_effects=True, vmem_limit_bytes=56 * 1024 * 1024
        ),
    )(*args)


def solution(mesh):
    rows = P(("group", "dom"), None)
    line = P(("group", "dom"))
    placed = (
        rows, P(), P(), P(), P(), P(), P(), P(), P(), P(),
        rows, line, P(("group", "dom"), None, None), rows, line,
    )
    return jax.shard_map(
        shards, mesh=mesh, in_specs=placed, out_specs=(rows, P()), check_vma=False
    )
```

time: 445 us -> 74.9 us (0.17); the launches traced: 437 us -> 74.7 us
  blocking collectives: 164 us -> 0 us
  local copies, waits for them, and re-layouts: 146 us -> 3.34 us
  Pallas kernels: 0 us -> 70.7 us
  waiting for transfers between devices: 55 us -> 0 us
  matrix products: 21.5 us -> 0 us
  other arithmetic: 17.7 us -> 0 us
  starting transfers between devices: 17.6 us -> 0 us
  between operations: 15.2 us -> 0.65 us
    pmax x1 -> x0, blocking collectives: 99.8 us -> none  [shards(): lax.pmax(jnp.max(member_masked, axis=2), ('group', 'dom'))]
    pallas_call x0 -> x1, Pallas kernels: none -> 70.7 us  [shards(): pl.pallas_call(kernel, out_shape=(jax.ShapeDtypeStruct((N, D), BF), jax.S...]
    gather x13 -> x0, local copies, waits for them, and re-layouts: 66.6 us -> none  [the longest x8 34.9 us: shards(): window[local_nbr[:, slot_idx]]]
    psum x1 -> x0, blocking collectives: 64.4 us -> none  [shards(): lax.psum((jnp.sum(v_raised, axis=2), part_acc), ('group', 'dom'))]
    psum x1 -> x0, waiting for transfers between devices: 54.9 us -> none  [shards(): lax.psum((jnp.sum(v_raised, axis=2), part_acc), ('group', 'dom'))]
    unnamed x86 -> x2, local copies, waits for them, and re-layouts: 53.1 us -> 3.34 us
    dot_general x10 -> x0, matrix products: 21.5 us -> none  [the longest x5 9.87 us: project(): jnp.dot(inputs, weight_one, preferred_element_type=jnp.float32)]
    slice x14 -> x0, local copies, waits for them, and re-layouts: 14.7 us -> none  [the longest x12 12.9 us: shards(): picked[:, :feat_width]]
  transfers between devices with their start and end apart: 4 -> 0, of which waited for: 1 -> 0; matrix products, arithmetic and copies ran while one was open for 25% -> 0% of each run, Pallas kernels for 0% -> 0%
where the time goes in v1:
time: 74.9 us; the launch traced here: 74.7 us
  Pallas kernels  70.7 us (94%)
  local copies, waits for them, and re-layouts  3.34 us (4%)
    pallas_call x1, Pallas kernels, shards(): pl.pallas_call(kernel, out_shape=(jax.ShapeDtypeStruct((N, D), BF), jax.S...  70.7 us
    unnamed x2, local copies, waits for them, and re-layouts  3.34 us

profile of v1, /device:TPU:1, one launch (start us, length us, event | category | flops | bytes accessed | tf_op | source)
XLA Modules:
  0.0 74.7 jit_solution(7098419142590420467)
XLA Ops:
  0.6 70.7 %shard_map.158 = (bf16[512,512]{1,0:T(8,128)(2,1)}, bf16[64,512]{1,0:T(8,128)(2,1)}) custom-call(bf16[512,512]{1,0:T(8,128)(2,1)} %x_hbm.1, bf16[64,512]{1,0:T(8,128)(2,1)} %vx_hbm.1, bf16[512,512]{1,0:T(8,128)(2,1)} %wq_hbm.1, bf16[512,512]{1,0:T(8,128)(2,1)} %wk_hbm.1, bf16[512,512]{1,0:T(8,128)(2,1)} %wv_hbm.1, bf16[512,512]{1,0:T(8,128)(2,1)} %wo_hbm.1, ...), custom_call_target="tpu_custom_call" | custom-call | tf_op jit(solution)/shard_map/pallas_call | solution.py:428
  71.4 1.9 %copy.19 = bf16[512,512]{1,0:T(8,128)(2,1)} copy(bf16[512,512]{1,0:T(8,128)(2,1)} %get-tuple-element.4) | data formatting | bytes 1048576
  73.2 1.5 %copy.20 = bf16[64,512]{1,0:T(8,128)(2,1)} copy(bf16[64,512]{1,0:T(8,128)(2,1)} %get-tuple-element.5) | data formatting | bytes 131072

commit v2 on v1

--- a/solution.py
+++ b/solution.py
@@ -27,6 +27,8 @@
 ROWS = BLOCKS * BLK
 EXP0 = FIRST_EXP * BLK
 PART = D + 256
+VR = HD + 16
+AR = HD + 8
 
 
 def dot(a, b, dims=((1,), (0,)), precision=None):
@@ -59,7 +61,7 @@
     nbr_hbm, len_hbm, rows_hbm, slot_hbm, mem_hbm,
     out_hbm, vout_hbm,
     xall, vx, wq, wk, wv, wo, wu, wd, ga, gf, nbr, length, rows, slot, mem,
-    send, wvt, qm, bias, kblk, vt, m_ref, l_ref, acc, att, outs,
+    send, wvt, qm, bias, kblk, vt, m_ref, acc, att, outs,
     vq32, vk32, vv32, vkey, vbias, part, r1, c1, r2, r3a, r3, vrow, vout,
     in_sem, out_sem, ssem, rsem, halo_s, halo_r, s1s, s1r, s2s, s2r, s3s, s3r, s4s, s4r,
 ):
@@ -120,31 +122,22 @@
     to_up.start()
     to_down.start()
 
+    tx = [wrap(x + i, 4) * 2 for i in range(4)]
+    tc = [c, 1 - c]
     ty = [wrap(y + i, 4) for i in range(4)]
-    tc = [c, 1 - c]
-
-    def post(group, kz, first):
-        kc, jx = group % 2, group // 2
-        tz = wrap(z + kz, 4)
-        xb = wrap(x + kz, 4)
-        for ky in range(first, 4):
-            tg = wrap(xb + (jx + ky) % 4, 4) * 2 + tc[kc]
-            td = tz * 4 + ty[ky]
-            pltpu.make_async_remote_copy(
-                send.at[pl.ds(pl.multiple_of((tg * 16 + td) * CAP, CAP), CAP)],
-                xall.at[pl.ds(pl.multiple_of(EXP0 + group * BLK + (kz * 4 + ky) * CAP, CAP), CAP)],
-                ssem, rsem.at[group], device_id=(tg, td), device_id_type=MESH,
-            ).start()
-
+    tz = [wrap(z + i, 4) * 4 for i in range(4)]
     for group in range(GROUPS):
-        if group == 0:
-            post(0, 0, 1)
-
-        def post_z(kz, carry):
-            post(group, kz, 0)
-            return carry
-
-        lax.fori_loop(1 if group == 0 else 0, 4, post_z, 0)
+        for kz in range(4):
+            for ky in range(4):
+                if group + kz + ky == 0:
+                    continue
+                tg = tx[(group // 2 + kz + ky) % 4] + tc[group % 2]
+                td = tz[kz] + ty[ky]
+                pltpu.make_async_remote_copy(
+                    send.at[pl.ds(pl.multiple_of((tg * 16 + td) * CAP, CAP), CAP)],
+                    xall.at[pl.ds(EXP0 + group * BLK + (kz * 4 + ky) * CAP, CAP)],
+                    ssem, rsem.at[group], device_id=(tg, td), device_id_type=MESH,
+                ).start()
     me = g * 16 + d
     xall[pl.ds(EXP0, CAP), :] = send[pl.ds(pl.multiple_of(me * CAP, CAP), CAP), :]
 
@@ -167,24 +160,33 @@
     member = iota((VN, N), 0) == member_row
     k_own = dot(xall[pl.ds(0, N), :], wk[...]).astype(BF)
     v_own = dot(xall[pl.ds(0, N), :], wv[...]).astype(BF)
-    head_of = iota((VN, D), 1) // HD
     lane = iota((VN, 128), 1)
-    part_acc = jnp.zeros((VN, D), F32)
     part_max = jnp.zeros((VN, 128), F32)
     part_sum = jnp.zeros((VN, 128), F32)
-    for h in range(H):
-        pair = slice(h // 2 * 128, h // 2 * 128 + 128)
-        vqh = jnp.where(head_of == h, vq32[...], 0.0).astype(BF)[:, pair]
-        s = jnp.where(member, dot(vqh, k_own[:, pair], NT), NEG)
-        top = jnp.max(s, axis=1, keepdims=True)
-        p = jnp.where(member, jnp.exp(s - top), 0.0)
-        part_max = jnp.where(lane == h, top, part_max)
-        part_sum = jnp.where(lane == h, jnp.sum(p, axis=1, keepdims=True), part_sum)
-        high = p.astype(BF)
-        low = (p - high.astype(F32)).astype(BF)
-        o = dot(high, v_own) + dot(low, v_own)
-        part_acc = jnp.where(head_of == h, o, part_acc)
-    part[:, pl.ds(0, D)] = part_acc
+    odd = iota((VN, 128), 1) >= HD
+    scored = []
+    for w in range(H // 2):
+        pair = slice(w * 128, w * 128 + 128)
+        vqp = vq32[:, pair]
+        vqp = jnp.concatenate([jnp.where(odd, 0.0, vqp), jnp.where(odd, vqp, 0.0)], axis=0)
+        scored.append(dot(vqp.astype(BF), k_own[:, pair], NT))
+    parts = []
+    for w in range(H // 2):
+        stack = []
+        for i in range(2):
+            s = jnp.where(member, scored[w][i * VN : (i + 1) * VN, :], NEG)
+            top = jnp.max(s, axis=1, keepdims=True)
+            p = jnp.where(member, jnp.exp(s - top), 0.0)
+            part_max = jnp.where(lane == 2 * w + i, top, part_max)
+            part_sum = jnp.where(lane == 2 * w + i, jnp.sum(p, axis=1, keepdims=True), part_sum)
+            high = p.astype(BF)
+            stack += [high, (p - high.astype(F32)).astype(BF)]
+        parts.append(jnp.concatenate(stack, axis=0))
+    for w in range(H // 2):
+        pair = slice(w * 128, w * 128 + 128)
+        o = dot(parts[w], v_own[:, pair])
+        even, uneven = o[:VN] + o[VN : 2 * VN], o[2 * VN : 3 * VN] + o[3 * VN :]
+        part[:, pair] = jnp.where(odd, uneven, even)
     part[:, pl.ds(D, 128)] = part_max
     part[:, pl.ds(D + 128, 128)] = part_sum
     for i in range(1, 8):
@@ -229,10 +231,11 @@
         pair = slice(h // 2 * 128, h // 2 * 128 + 128)
         s = dot(vkey[:, pair], qm[h], NT) + vbias[...]
         top = jnp.max(s, axis=0, keepdims=True)
-        p = jnp.exp(s - top)
         m_ref[h : h + 1, :] = top
-        l_ref[h : h + 1, :] = jnp.sum(p, axis=0, keepdims=True)
-        acc[h * HD : (h + 1) * HD, :] = dot(vvt[h * HD : (h + 1) * HD, :], p.astype(BF))
+        p = jnp.exp((s - top).astype(BF))
+        vals = jnp.concatenate([vvt[h * HD : (h + 1) * HD, :], jnp.ones((VR - HD, VN), BF)], axis=0)
+        acc[h] = dot(vals, p)[:AR, :]
+        vt[h, pl.ds(HD, VR - HD), :] = jnp.ones((VR - HD, BLK), BF)
 
     def wait_bytes(like, sem):
         pltpu.make_async_copy(like, like, sem).wait()
@@ -329,18 +332,21 @@
         r = pl.multiple_of(b * BLK, BLK)
         xb = xall[pl.ds(r, BLK), :]
         kblk[...] = dot(xb, wk[...]).astype(BF)
-        vt[...] = dot(wvt[...], xb, NT).astype(BF)
+        vals = dot(wvt[...], xb, NT).astype(BF)
         for h in range(H):
-            pair = slice(h // 2 * 128, h // 2 * 128 + 128)
-            s = dot(kblk[:, pair], qm[h], NT) + bias[pl.ds(r, BLK), :]
+            vt[h, pl.ds(0, HD), :] = vals[h * HD : (h + 1) * HD, :]
+        add = bias[pl.ds(r, BLK), :]
+        scored = [dot(kblk[:, h // 2 * 128 : h // 2 * 128 + 128], qm[h], NT) for h in range(H)]
+        weighed = []
+        for h in range(H):
+            s = scored[h] + add
             old = m_ref[h : h + 1, :]
             top = jnp.maximum(old, jnp.max(s, axis=0, keepdims=True))
-            keep = jnp.exp(old - top)
-            p = jnp.exp(s - top)
             m_ref[h : h + 1, :] = top
-            l_ref[h : h + 1, :] = l_ref[h : h + 1, :] * keep + jnp.sum(p, axis=0, keepdims=True)
-            span = slice(h * HD, (h + 1) * HD)
-            acc[span, :] = acc[span, :] * keep + dot(vt[span, :], p.astype(BF))
+            weighed.append((jnp.exp((s - top).astype(BF)), jnp.exp(old - top)))
+        for h in range(H):
+            p, keep = weighed[h]
+            acc[h] = acc[h] * keep + dot(vt[h], p)[:AR, :]
         return carry
 
     def vx_row(v):
@@ -351,7 +357,7 @@
 
     for h in range(H):
         span = slice(h * HD, (h + 1) * HD)
-        att[span, :] = (acc[span, :] * (1.0 / l_ref[h : h + 1, :])).astype(BF)
+        att[span, :] = (acc[h, :HD, :] * (1.0 / acc[h, HD : HD + 1, :])).astype(BF)
     loads[13].wait()
     loads[14].wait()
     attn = att[...].T
@@ -396,6 +402,17 @@
 def vx32_row(vx, v):
     hot = (iota((8, VN), 1) == v).astype(F32).astype(BF)
     return dot(hot, vx[...])[0:1, :]
+
+
+def hand_over(node, virtual, node_out, virtual_out, sem):
+    copies = [pltpu.make_async_copy(virtual, virtual_out, sem.at[4])]
+    for i in range(4):
+        at = pl.ds(i * 128, 128)
+        copies.append(pltpu.make_async_copy(node.at[at], node_out.at[at], sem.at[i]))
+    for copy in copies:
+        copy.start()
+    for copy in copies:
+        copy.wait()
 
 
 def shards(
@@ -415,8 +432,8 @@
         vmem((1, D), F32), vmem((1, D), F32), vmem((8, N), jnp.int32), vmem((1, N), jnp.int32),
         vmem((CAP, 128), jnp.int32), vmem((4, N), jnp.int32), vmem((1, N), jnp.int32),
         vmem((128 * CAP, D), BF), vmem((D, D), BF), vmem((H, N, 128), BF), vmem((ROWS, N), F32),
-        vmem((BLK, D), BF), vmem((D, BLK), BF), vmem((H, N), F32), vmem((H, N), F32),
-        vmem((D, N), F32), vmem((D, N), BF), vmem((N, D), BF),
+        vmem((BLK, D), BF), vmem((H, VR, BLK), BF), vmem((H, N), F32),
+        vmem((H, AR, N), F32), vmem((D, N), BF), vmem((N, D), BF),
         vmem((VN, D), F32), vmem((VN, D), F32), vmem((VN, D), F32), vmem((VN, D), BF),
         vmem((VN, N), F32), vmem((VN, PART), F32), vmem((8, 8, PART), F32),
         vmem((8, 1, PART), F32), vmem((16, 1, PART), F32), vmem((8, 1, D), F32),
@@ -425,7 +442,7 @@
         dma, dma, dma, dma, dma, dma, dma, dma,
     ]
     hbm = pl.BlockSpec(memory_space=pl.ANY)
-    return pl.pallas_call(
+    node, virtual = pl.pallas_call(
         kernel,
         out_shape=(
             jax.ShapeDtypeStruct((N, D), BF),
@@ -438,6 +455,17 @@
             collective_id=0, has_side_effects=True, vmem_limit_bytes=56 * 1024 * 1024
         ),
     )(*args)
+    return pl.pallas_call(
+        hand_over,
+        out_shape=(
+            jax.ShapeDtypeStruct((N, D), BF),
+            jax.ShapeDtypeStruct((VN, D), BF),
+        ),
+        in_specs=[hbm] * 2,
+        out_specs=(hbm, hbm),
+        scratch_shapes=[dma((5,))],
+        compiler_params=pltpu.CompilerParams(vmem_limit_bytes=60 * 1024 * 1024),
+    )(node, virtual)
 
 
 def solution(mesh):

time: 74.9 us -> 79.8 us (1.065)
  Pallas kernels: 70.7 us -> 79.1 us
  local copies, waits for them, and re-layouts: 3.34 us -> 0 us
    pallas_call x0 -> x1, Pallas kernels: none -> 19 us  [shards(): pl.pallas_call(hand_over, out_shape=(jax.ShapeDtypeStruct((N, D), BF), ja...]
    pallas_call x1, Pallas kernels: 70.7 us -> 60 us  [shards(): pl.pallas_call(kernel, out_shape=(jax.ShapeDtypeStruct((N, D), BF), jax.S...]
    unnamed x2 -> x0, local copies, waits for them, and re-layouts: 3.34 us -> none
where the time goes in v2:
time: 79.8 us; the launch traced here: 79.7 us
  Pallas kernels  79.1 us (99%)
    pallas_call x1, Pallas kernels, shards(): pl.pallas_call(kernel, out_shape=(jax.ShapeDtypeStruct((N, D), BF), jax.S...  60 us
    pallas_call x1, Pallas kernels, shards(): pl.pallas_call(hand_over, out_shape=(jax.ShapeDtypeStruct((N, D), BF), ja...  19 us

profile of v2, /device:TPU:1, one launch (start us, length us, event | category | flops | bytes accessed | tf_op | source)
XLA Modules:
  0.0 79.7 jit_solution(9322168487292814488)
XLA Ops:
  0.6 60.0 %shard_map.158 = (bf16[512,512]{1,0:T(8,128)(2,1)}, bf16[64,512]{1,0:T(8,128)(2,1)}) custom-call(bf16[512,512]{1,0:T(8,128)(2,1)} %x_hbm.1, bf16[64,512]{1,0:T(8,128)(2,1)} %vx_hbm.1, bf16[512,512]{1,0:T(8,128)(2,1)} %wq_hbm.1, bf16[512,512]{1,0:T(8,128)(2,1)} %wk_hbm.1, bf16[512,512]{1,0:T(8,128)(2,1)} %wv_hbm.1, bf16[512,512]{1,0:T(8,128)(2,1)} %wo_hbm.1, ...), custom_call_target="tpu_custom_call" | custom-call | tf_op jit(solution)/shard_map/pallas_call | solution.py:445
  60.7 19.0 %shard_map.159 = (bf16[512,512]{1,0:T(8,128)(2,1)}, bf16[64,512]{1,0:T(8,128)(2,1)}) custom-call(bf16[512,512]{1,0:T(8,128)(2,1)} %get-tuple-element.4.node, bf16[64,512]{1,0:T(8,128)(2,1)} %get-tuple-element.5.virtual), custom_call_target="tpu_custom_call" | custom-call | tf_op jit(solution)/shard_map/pallas_call | solution.py:458

commit v3 on v2

--- a/solution.py
+++ b/solution.py
@@ -404,15 +404,20 @@
     return dot(hot, vx[...])[0:1, :]
 
 
-def hand_over(node, virtual, node_out, virtual_out, sem):
-    copies = [pltpu.make_async_copy(virtual, virtual_out, sem.at[4])]
+def hand_over(node, virtual, node_out, virtual_out, held, vheld, sem):
+    steps = [(virtual, vheld, virtual_out)]
     for i in range(4):
         at = pl.ds(i * 128, 128)
-        copies.append(pltpu.make_async_copy(node.at[at], node_out.at[at], sem.at[i]))
-    for copy in copies:
-        copy.start()
-    for copy in copies:
-        copy.wait()
+        steps.append((node.at[at], held.at[at], node_out.at[at]))
+    loads = [pltpu.make_async_copy(a, b, sem.at[0, i]) for i, (a, b, _) in enumerate(steps)]
+    stores = [pltpu.make_async_copy(b, c, sem.at[1, i]) for i, (_, b, c) in enumerate(steps)]
+    for load in loads:
+        load.start()
+    for load, store in zip(loads, stores):
+        load.wait()
+        store.start()
+    for store in stores:
+        store.wait()
 
 
 def shards(
@@ -463,7 +468,7 @@
         ),
         in_specs=[hbm] * 2,
         out_specs=(hbm, hbm),
-        scratch_shapes=[dma((5,))],
+        scratch_shapes=[vmem((N, D), BF), vmem((VN, D), BF), dma((2, 5))],
         compiler_params=pltpu.CompilerParams(vmem_limit_bytes=60 * 1024 * 1024),
     )(node, virtual)
 

time: 79.8 us -> 62.7 us (0.79)
  Pallas kernels: 79.1 us -> 61.9 us
    pallas_call x1, Pallas kernels: 19 us -> 1.87 us  [shards(): pl.pallas_call(hand_over, out_shape=(jax.ShapeDtypeStruct((N, D), BF), ja...]
where the time goes in v3:
time: 62.7 us; the launch traced here: 62.6 us
  Pallas kernels  61.9 us (99%)
  between operations  0.64 us (1%)
    pallas_call x1, Pallas kernels, shards(): pl.pallas_call(kernel, out_shape=(jax.ShapeDtypeStruct((N, D), BF), jax.S...  60 us
    pallas_call x1, Pallas kernels, shards(): pl.pallas_call(hand_over, out_shape=(jax.ShapeDtypeStruct((N, D), BF), ja...  1.87 us

profile of v3, /device:TPU:1, one launch (start us, length us, event | category | flops | bytes accessed | tf_op | source)
XLA Modules:
  0.0 62.6 jit_solution(11538799205059107096)
XLA Ops:
  0.6 60.0 %shard_map.158 = (bf16[512,512]{1,0:T(8,128)(2,1)}, bf16[64,512]{1,0:T(8,128)(2,1)}) custom-call(bf16[512,512]{1,0:T(8,128)(2,1)} %x_hbm.1, bf16[64,512]{1,0:T(8,128)(2,1)} %vx_hbm.1, bf16[512,512]{1,0:T(8,128)(2,1)} %wq_hbm.1, bf16[512,512]{1,0:T(8,128)(2,1)} %wk_hbm.1, bf16[512,512]{1,0:T(8,128)(2,1)} %wv_hbm.1, bf16[512,512]{1,0:T(8,128)(2,1)} %wo_hbm.1, ...), custom_call_target="tpu_custom_call" | custom-call | tf_op jit(solution)/shard_map/pallas_call | solution.py:450
  60.7 1.9 %shard_map.159 = (bf16[512,512]{1,0:T(8,128)(2,1)}, bf16[64,512]{1,0:T(8,128)(2,1)}) custom-call(bf16[512,512]{1,0:T(8,128)(2,1)} %get-tuple-element.4.node, bf16[64,512]{1,0:T(8,128)(2,1)} %get-tuple-element.5.virtual), custom_call_target="tpu_custom_call" | custom-call | tf_op jit(solution)/shard_map/pallas_call | solution.py:463

commit v4 on v3

--- a/solution.py
+++ b/solution.py
@@ -107,39 +107,6 @@
             axis=0,
         )
         send[pl.ds(chunk * 256, 256), :] = dot(hot, xall[pl.ds(0, N), :]).astype(BF)
-
-    pl.semaphore_wait(barrier, 127)
-
-    up, down = wrap(d + 1, 16), wrap(d + 15, 16)
-    to_up = pltpu.make_async_remote_copy(
-        xall.at[pl.ds(N - HALO, HALO)], xall.at[pl.ds(N + HALO, HALO)],
-        halo_s.at[0], halo_r.at[0], device_id=(g, up), device_id_type=MESH,
-    )
-    to_down = pltpu.make_async_remote_copy(
-        xall.at[pl.ds(0, HALO)], xall.at[pl.ds(N, HALO)],
-        halo_s.at[1], halo_r.at[1], device_id=(g, down), device_id_type=MESH,
-    )
-    to_up.start()
-    to_down.start()
-
-    tx = [wrap(x + i, 4) * 2 for i in range(4)]
-    tc = [c, 1 - c]
-    ty = [wrap(y + i, 4) for i in range(4)]
-    tz = [wrap(z + i, 4) * 4 for i in range(4)]
-    for group in range(GROUPS):
-        for kz in range(4):
-            for ky in range(4):
-                if group + kz + ky == 0:
-                    continue
-                tg = tx[(group // 2 + kz + ky) % 4] + tc[group % 2]
-                td = tz[kz] + ty[ky]
-                pltpu.make_async_remote_copy(
-                    send.at[pl.ds(pl.multiple_of((tg * 16 + td) * CAP, CAP), CAP)],
-                    xall.at[pl.ds(EXP0 + group * BLK + (kz * 4 + ky) * CAP, CAP)],
-                    ssem, rsem.at[group], device_id=(tg, td), device_id_type=MESH,
-                ).start()
-    me = g * 16 + d
-    xall[pl.ds(EXP0, CAP), :] = send[pl.ds(pl.multiple_of(me * CAP, CAP), CAP), :]
 
     for i in range(2, 12):
         loads[i].wait()
@@ -189,12 +156,48 @@
         part[:, pair] = jnp.where(odd, uneven, even)
     part[:, pl.ds(D, 128)] = part_max
     part[:, pl.ds(D + 128, 128)] = part_sum
+    pl.semaphore_wait(barrier, 127)
     for i in range(1, 8):
         pltpu.make_async_remote_copy(
             part.at[pl.ds(pl.multiple_of(others[i] * 8, 8), 8)], r1.at[g],
             s1s, s1r, device_id=(others[i], d), device_id_type=MESH,
         ).start()
     r1[g] = part[pl.ds(pl.multiple_of(g * 8, 8), 8), :]
+
+    up, down = wrap(d + 1, 16), wrap(d + 15, 16)
+    to_up = pltpu.make_async_remote_copy(
+        xall.at[pl.ds(N - HALO, HALO)], xall.at[pl.ds(N + HALO, HALO)],
+        halo_s.at[0], halo_r.at[0], device_id=(g, up), device_id_type=MESH,
+    )
+    to_down = pltpu.make_async_remote_copy(
+        xall.at[pl.ds(0, HALO)], xall.at[pl.ds(N, HALO)],
+        halo_s.at[1], halo_r.at[1], device_id=(g, down), device_id_type=MESH,
+    )
+    to_up.start()
+    to_down.start()
+
+    tx = [wrap(x + i, 4) * 2 for i in range(4)]
+    tc = [c, 1 - c]
+    ty = [wrap(y + i, 4) for i in range(4)]
+    tz = [wrap(z + i, 4) * 4 for i in range(4)]
+
+    def post(group):
+        for kz in range(4):
+            for ky in range(4):
+                if group + kz + ky == 0:
+                    continue
+                tg = tx[(group // 2 + kz + ky) % 4] + tc[group % 2]
+                td = tz[kz] + ty[ky]
+                pltpu.make_async_remote_copy(
+                    send.at[pl.ds(pl.multiple_of((tg * 16 + td) * CAP, CAP), CAP)],
+                    xall.at[pl.ds(EXP0 + group * BLK + (kz * 4 + ky) * CAP, CAP)],
+                    ssem, rsem.at[group], device_id=(tg, td), device_id_type=MESH,
+                ).start()
+
+    post(0)
+    post(1)
+    me = g * 16 + d
+    xall[pl.ds(EXP0, CAP), :] = send[pl.ds(pl.multiple_of(me * CAP, CAP), CAP), :]
 
     win = nbr[...] - HALO
     win = jnp.where(win < 0, win + EXP0, win)
@@ -227,15 +230,19 @@
 
     vvt = vval.T
     vbias[...] = jnp.where(member, 0.0, NEG)
+    add = vbias[...]
+    scored = [dot(vkey[:, h // 2 * 128 : h // 2 * 128 + 128], qm[h], NT) for h in range(H)]
+    weighed = []
     for h in range(H):
-        pair = slice(h // 2 * 128, h // 2 * 128 + 128)
-        s = dot(vkey[:, pair], qm[h], NT) + vbias[...]
+        s = scored[h] + add
         top = jnp.max(s, axis=0, keepdims=True)
         m_ref[h : h + 1, :] = top
-        p = jnp.exp((s - top).astype(BF))
-        vals = jnp.concatenate([vvt[h * HD : (h + 1) * HD, :], jnp.ones((VR - HD, VN), BF)], axis=0)
-        acc[h] = dot(vals, p)[:AR, :]
-        vt[h, pl.ds(HD, VR - HD), :] = jnp.ones((VR - HD, BLK), BF)
+        weighed.append(jnp.exp((s - top).astype(BF)))
+    ones = jnp.ones((VR - HD, BLK), BF)
+    for h in range(H):
+        vals = jnp.concatenate([vvt[h * HD : (h + 1) * HD, :], ones[:, :VN]], axis=0)
+        acc[h] = dot(vals, weighed[h])[:AR, :]
+        vt[h, pl.ds(HD, VR - HD), :] = ones
 
     def wait_bytes(like, sem):
         pltpu.make_async_copy(like, like, sem).wait()
@@ -255,20 +262,7 @@
         return mixed, top, total
 
     def block(b, carry):
-        @pl.when(b == OWN_BLOCKS)
-        def _():
-            to_up.wait_recv()
-            to_down.wait_recv()
-
-        @pl.when(b == FIRST_EXP)
-        def _():
-            wait_bytes(xall.at[pl.ds(EXP0, 15 * CAP)], rsem.at[0])
-
-        @pl.when(b > FIRST_EXP)
-        def _():
-            wait_bytes(xall.at[pl.ds(EXP0, 16 * CAP)], rsem.at[b - FIRST_EXP])
-
-        @pl.when(b == FIRST_EXP)
+        @pl.when(b == 0)
         def _():
             wait_bytes(r1.at[pl.ds(0, 7)], s1r)
             mixed, top, total = combine([r1[i] for i in range(8)])
@@ -288,7 +282,12 @@
             def _():
                 r2[d] = c1[d]
 
-        @pl.when((b == FIRST_EXP + 2) & (d < 8))
+        @pl.when(b == 0)
+        def _():
+            post(2)
+            post(3)
+
+        @pl.when((b == OWN_BLOCKS) & (d < 8))
         def _():
             wait_bytes(r2.at[pl.ds(0, 15)], s2r)
             mixed, top, total = combine([r2[i] for i in range(16)])
@@ -313,7 +312,12 @@
                 ).start()
             r3a[d] = vrow[0]
 
-        @pl.when(b == FIRST_EXP + 5)
+        @pl.when(b == OWN_BLOCKS)
+        def _():
+            post(4)
+            post(5)
+
+        @pl.when(b == FIRST_EXP + 1)
         def _():
             @pl.when(d < 8)
             def _():
@@ -328,6 +332,24 @@
                 pltpu.make_async_remote_copy(
                     r3.at[g], r3.at[g], s4s, s4r, device_id=(others[i], d), device_id_type=MESH
                 ).start()
+
+        @pl.when(b == FIRST_EXP + 1)
+        def _():
+            post(6)
+            post(7)
+
+        @pl.when(b == OWN_BLOCKS)
+        def _():
+            to_up.wait_recv()
+            to_down.wait_recv()
+
+        @pl.when(b == FIRST_EXP)
+        def _():
+            wait_bytes(xall.at[pl.ds(EXP0, 15 * CAP)], rsem.at[0])
+
+        @pl.when(b > FIRST_EXP)
+        def _():
+            wait_bytes(xall.at[pl.ds(EXP0, 16 * CAP)], rsem.at[b - FIRST_EXP])
 
         r = pl.multiple_of(b * BLK, BLK)
         xb = xall[pl.ds(r, BLK), :]
@@ -355,28 +377,27 @@
     loads[12].wait()
     lax.fori_loop(0, BLOCKS, block, 0)
 
+    wait_bytes(r3.at[pl.ds(0, 7)], s4r)
+    vout[...] = r3[...].reshape(VN, D).astype(BF)
+    last = pltpu.make_async_copy(vout, vout_hbm, out_sem.at[2])
+    last.start()
+
     for h in range(H):
         span = slice(h * HD, (h + 1) * HD)
         att[span, :] = (acc[h, :HD, :] * (1.0 / acc[h, HD : HD + 1, :])).astype(BF)
     loads[13].wait()
     loads[14].wait()
-    attn = att[...].T
-    att[...] = attn
-    for r in range(0, N, BLK):
-        at = pl.ds(r, BLK)
+    att[...] = att[...].T
+    chunks = [pl.ds(r, BLK) for r in range(0, N, BLK)]
+    settled = []
+    for at in chunks:
         mixed = xall[at, :].astype(F32) + dot(att[at, :], wo[...])
-        settled = norm(mixed, ga[...]).astype(BF)
-        total = settled.astype(F32)
-        for f in range(0, 4 * D, D):
-            hidden = jnp.maximum(dot(settled, wu[:, f : f + D]), 0.0).astype(BF)
-            total = total + dot(hidden, wd[f : f + D, :])
+        settled.append(norm(mixed, ga[...]).astype(BF))
+    for i, at in enumerate(chunks):
+        hidden = jnp.maximum(dot(settled[i], wu[...]), 0.0).astype(BF)
+        total = settled[i].astype(F32) + dot(hidden, wd[...])
         outs[at, :] = norm(total, gf[...]).astype(BF)
-        pltpu.make_async_copy(outs.at[at], out_hbm.at[at], out_sem.at[r // BLK]).start()
-
-    wait_bytes(r3.at[pl.ds(0, 7)], s4r)
-    vout[...] = r3[...].reshape(VN, D).astype(BF)
-    last = pltpu.make_async_copy(vout, vout_hbm, out_sem.at[2])
-    last.start()
+        pltpu.make_async_copy(outs.at[at], out_hbm.at[at], out_sem.at[i]).start()
 
     to_up.wait_send()
     to_down.wait_send()

time: 62.7 us -> 54.3 us (0.87)
  the two profiles are of different devices: /device:TPU:1 before, /device:TPU:0 now
where the time goes in v4:
time: 54.3 us; the launch traced here: 54.2 us
  Pallas kernels  53.5 us (99%)
  between operations  0.64 us (1%)
    pallas_call x1, Pallas kernels, shards(): pl.pallas_call(kernel, out_shape=(jax.ShapeDtypeStruct((N, D), BF), jax.S...  51.7 us
    pallas_call x1, Pallas kernels, shards(): pl.pallas_call(hand_over, out_shape=(jax.ShapeDtypeStruct((N, D), BF), ja...  1.87 us

profile of v4, /device:TPU:0, one launch (start us, length us, event | category | flops | bytes accessed | tf_op | source)
XLA Modules:
  0.0 54.2 jit_solution(10368276755263926535)
XLA Ops:
  0.6 51.7 %shard_map.158 = (bf16[512,512]{1,0:T(8,128)(2,1)}, bf16[64,512]{1,0:T(8,128)(2,1)}) custom-call(bf16[512,512]{1,0:T(8,128)(2,1)} %x_hbm.1, bf16[64,512]{1,0:T(8,128)(2,1)} %vx_hbm.1, bf16[512,512]{1,0:T(8,128)(2,1)} %wq_hbm.1, bf16[512,512]{1,0:T(8,128)(2,1)} %wk_hbm.1, bf16[512,512]{1,0:T(8,128)(2,1)} %wv_hbm.1, bf16[512,512]{1,0:T(8,128)(2,1)} %wo_hbm.1, ...), custom_call_target="tpu_custom_call" | custom-call | tf_op jit(solution)/shard_map/pallas_call | solution.py:471
  52.3 1.9 %shard_map.159 = (bf16[512,512]{1,0:T(8,128)(2,1)}, bf16[64,512]{1,0:T(8,128)(2,1)}) custom-call(bf16[512,512]{1,0:T(8,128)(2,1)} %get-tuple-element.4.node, bf16[64,512]{1,0:T(8,128)(2,1)} %get-tuple-element.5.virtual), custom_call_target="tpu_custom_call" | custom-call | tf_op jit(solution)/shard_map/pallas_call | solution.py:484

commit v5 on v2

--- a/solution.py
+++ b/solution.py
@@ -29,6 +29,8 @@
 PART = D + 256
 VR = HD + 16
 AR = HD + 8
+AHEAD = 6
+FIRST = 2
 
 
 def dot(a, b, dims=((1,), (0,)), precision=None):
@@ -59,11 +61,11 @@
 def kernel(
     x_hbm, vx_hbm, wq_hbm, wk_hbm, wv_hbm, wo_hbm, wu_hbm, wd_hbm, ga_hbm, gf_hbm,
     nbr_hbm, len_hbm, rows_hbm, slot_hbm, mem_hbm,
-    out_hbm, vout_hbm,
+    outs, vout,
     xall, vx, wq, wk, wv, wo, wu, wd, ga, gf, nbr, length, rows, slot, mem,
-    send, wvt, qm, bias, kblk, vt, m_ref, acc, att, outs,
-    vq32, vk32, vv32, vkey, vbias, part, r1, c1, r2, r3a, r3, vrow, vout,
-    in_sem, out_sem, ssem, rsem, halo_s, halo_r, s1s, s1r, s2s, s2r, s3s, s3r, s4s, s4r,
+    send, wvt, qm, bias, kblk, vt, m_ref, acc, att,
+    vq32, vk32, vv32, vkey, vbias, part, r1, c1, r2, r3a, r3, vrow,
+    in_sem, ssem, rsem, halo_s, halo_r, s1s, s1r, s2s, s2r, s3s, s3r, s4s, s4r,
 ):
     g = lax.axis_index("group")
     d = lax.axis_index("dom")
@@ -108,8 +110,6 @@
         )
         send[pl.ds(chunk * 256, 256), :] = dot(hot, xall[pl.ds(0, N), :]).astype(BF)
 
-    pl.semaphore_wait(barrier, 127)
-
     up, down = wrap(d + 1, 16), wrap(d + 15, 16)
     to_up = pltpu.make_async_remote_copy(
         xall.at[pl.ds(N - HALO, HALO)], xall.at[pl.ds(N + HALO, HALO)],
@@ -119,14 +119,13 @@
         xall.at[pl.ds(0, HALO)], xall.at[pl.ds(N, HALO)],
         halo_s.at[1], halo_r.at[1], device_id=(g, down), device_id_type=MESH,
     )
-    to_up.start()
-    to_down.start()
 
     tx = [wrap(x + i, 4) * 2 for i in range(4)]
     tc = [c, 1 - c]
     ty = [wrap(y + i, 4) for i in range(4)]
     tz = [wrap(z + i, 4) * 4 for i in range(4)]
-    for group in range(GROUPS):
+
+    def post(group):
         for kz in range(4):
             for ky in range(4):
                 if group + kz + ky == 0:
@@ -138,8 +137,19 @@
                     xall.at[pl.ds(EXP0 + group * BLK + (kz * 4 + ky) * CAP, CAP)],
                     ssem, rsem.at[group], device_id=(tg, td), device_id_type=MESH,
                 ).start()
-    me = g * 16 + d
-    xall[pl.ds(EXP0, CAP), :] = send[pl.ds(pl.multiple_of(me * CAP, CAP), CAP), :]
+
+    late = jnp.minimum(x, 2) + jnp.minimum(y, 2) + z >= 5
+
+    def begin():
+        to_up.start()
+        to_down.start()
+        for group in range(FIRST):
+            post(group)
+
+    @pl.when(late)
+    def _():
+        pl.semaphore_wait(barrier, 127)
+        begin()
 
     for i in range(2, 12):
         loads[i].wait()
@@ -189,12 +199,26 @@
         part[:, pair] = jnp.where(odd, uneven, even)
     part[:, pl.ds(D, 128)] = part_max
     part[:, pl.ds(D + 128, 128)] = part_sum
+
+    @pl.when(jnp.logical_not(late))
+    def _():
+        pl.semaphore_wait(barrier, 127)
+
     for i in range(1, 8):
         pltpu.make_async_remote_copy(
             part.at[pl.ds(pl.multiple_of(others[i] * 8, 8), 8)], r1.at[g],
             s1s, s1r, device_id=(others[i], d), device_id_type=MESH,
         ).start()
     r1[g] = part[pl.ds(pl.multiple_of(g * 8, 8), 8), :]
+
+    @pl.when(jnp.logical_not(late))
+    def _():
+        begin()
+
+    for group in range(FIRST, AHEAD):
+        post(group)
+    me = g * 16 + d
+    xall[pl.ds(EXP0, CAP), :] = send[pl.ds(pl.multiple_of(me * CAP, CAP), CAP), :]
 
     win = nbr[...] - HALO
     win = jnp.where(win < 0, win + EXP0, win)
@@ -227,15 +251,19 @@
 
     vvt = vval.T
     vbias[...] = jnp.where(member, 0.0, NEG)
+    add = vbias[...]
+    scored = [dot(vkey[:, h // 2 * 128 : h // 2 * 128 + 128], qm[h], NT) for h in range(H)]
+    weighed = []
     for h in range(H):
-        pair = slice(h // 2 * 128, h // 2 * 128 + 128)
-        s = dot(vkey[:, pair], qm[h], NT) + vbias[...]
+        s = scored[h] + add
         top = jnp.max(s, axis=0, keepdims=True)
         m_ref[h : h + 1, :] = top
-        p = jnp.exp((s - top).astype(BF))
-        vals = jnp.concatenate([vvt[h * HD : (h + 1) * HD, :], jnp.ones((VR - HD, VN), BF)], axis=0)
-        acc[h] = dot(vals, p)[:AR, :]
-        vt[h, pl.ds(HD, VR - HD), :] = jnp.ones((VR - HD, BLK), BF)
+        weighed.append(jnp.exp((s - top).astype(BF)))
+    ones = jnp.ones((VR - HD, BLK), BF)
+    for h in range(H):
+        vals = jnp.concatenate([vvt[h * HD : (h + 1) * HD, :], ones[:, :VN]], axis=0)
+        acc[h] = dot(vals, weighed[h])[:AR, :]
+        vt[h, pl.ds(HD, VR - HD), :] = ones
 
     def wait_bytes(like, sem):
         pltpu.make_async_copy(like, like, sem).wait()
@@ -255,20 +283,7 @@
         return mixed, top, total
 
     def block(b, carry):
-        @pl.when(b == OWN_BLOCKS)
-        def _():
-            to_up.wait_recv()
-            to_down.wait_recv()
-
-        @pl.when(b == FIRST_EXP)
-        def _():
-            wait_bytes(xall.at[pl.ds(EXP0, 15 * CAP)], rsem.at[0])
-
-        @pl.when(b > FIRST_EXP)
-        def _():
-            wait_bytes(xall.at[pl.ds(EXP0, 16 * CAP)], rsem.at[b - FIRST_EXP])
-
-        @pl.when(b == FIRST_EXP)
+        @pl.when(b == 0)
         def _():
             wait_bytes(r1.at[pl.ds(0, 7)], s1r)
             mixed, top, total = combine([r1[i] for i in range(8)])
@@ -278,21 +293,21 @@
                 c1[i, :, pl.ds(D + 128, 128)] = total[i : i + 1, :]
 
             for i in range(8):
-                @pl.when(d != i)
+                @pl.when(d != i + 8)
                 def _():
                     pltpu.make_async_remote_copy(
-                        c1.at[i], r2.at[d], s2s, s2r, device_id=(g, i), device_id_type=MESH
+                        c1.at[i], r2.at[d], s2s, s2r, device_id=(g, i + 8), device_id_type=MESH
                     ).start()
 
-            @pl.when(d < 8)
+            @pl.when(d >= 8)
             def _():
-                r2[d] = c1[d]
-
-        @pl.when((b == FIRST_EXP + 2) & (d < 8))
+                r2[d] = c1[d - 8]
+
+        @pl.when((b == FIRST_EXP + 6) & (d >= 8))
         def _():
             wait_bytes(r2.at[pl.ds(0, 15)], s2r)
             mixed, top, total = combine([r2[i] for i in range(16)])
-            v = g * 8 + d
+            v = g * 8 + d - 8
             vq, vk, vv = vq32[pl.ds(v, 1), :], vk32[pl.ds(v, 1), :], vv32[pl.ds(v, 1), :]
             eight = lambda row: jnp.broadcast_to(row, (8, row.shape[1]))
             own = dot(eight(vq * vk), expand, NT, precision=lax.Precision.HIGHEST)[0:1, :]
@@ -308,26 +323,31 @@
             vrow[0] = norm(u, ga[...]).astype(BF).astype(F32)[0:1, :]
             for i in range(1, 16):
                 pltpu.make_async_remote_copy(
-                    vrow.at[0], r3a.at[d], s3s, s3r,
+                    vrow.at[0], r3a.at[d - 8], s3s, s3r,
                     device_id=(g, wrap(d + i, 16)), device_id_type=MESH,
                 ).start()
-            r3a[d] = vrow[0]
-
-        @pl.when(b == FIRST_EXP + 5)
-        def _():
-            @pl.when(d < 8)
-            def _():
-                wait_bytes(r3a.at[pl.ds(0, 7)], s3r)
-
-            @pl.when(d >= 8)
-            def _():
-                wait_bytes(r3a.at[pl.ds(0, 8)], s3r)
-
-            r3[g] = r3a[:, 0, :]
-            for i in range(1, 8):
-                pltpu.make_async_remote_copy(
-                    r3.at[g], r3.at[g], s4s, s4r, device_id=(others[i], d), device_id_type=MESH
-                ).start()
+            r3a[d - 8] = vrow[0]
+
+        @pl.when(b == OWN_BLOCKS)
+        def _():
+            to_up.wait_recv()
+            to_down.wait_recv()
+
+        @pl.when(b == FIRST_EXP)
+        def _():
+            wait_bytes(xall.at[pl.ds(EXP0, 15 * CAP)], rsem.at[0])
+
+        @pl.when(b > FIRST_EXP)
+        def _():
+            wait_bytes(xall.at[pl.ds(EXP0, 16 * CAP)], rsem.at[b - FIRST_EXP])
+
+        @pl.when(b == FIRST_EXP + 0)
+        def _():
+            post(AHEAD + 0)
+
+        @pl.when(b == FIRST_EXP + 1)
+        def _():
+            post(AHEAD + 1)
 
         r = pl.multiple_of(b * BLK, BLK)
         xb = xall[pl.ds(r, BLK), :]
@@ -355,28 +375,38 @@
     loads[12].wait()
     lax.fori_loop(0, BLOCKS, block, 0)
 
+    @pl.when(d < 8)
+    def _():
+        wait_bytes(r3a, s3r)
+
+    @pl.when(d >= 8)
+    def _():
+        wait_bytes(r3a.at[pl.ds(0, 7)], s3r)
+
+    r3[g] = r3a[:, 0, :]
+    for i in range(1, 8):
+        pltpu.make_async_remote_copy(
+            r3.at[g], r3.at[g], s4s, s4r, device_id=(others[i], d), device_id_type=MESH
+        ).start()
+
     for h in range(H):
         span = slice(h * HD, (h + 1) * HD)
         att[span, :] = (acc[h, :HD, :] * (1.0 / acc[h, HD : HD + 1, :])).astype(BF)
     loads[13].wait()
     loads[14].wait()
-    attn = att[...].T
-    att[...] = attn
-    for r in range(0, N, BLK):
-        at = pl.ds(r, BLK)
+    att[...] = att[...].T
+    chunks = [pl.ds(r, BLK) for r in range(0, N, BLK)]
+    settled = []
+    for at in chunks:
         mixed = xall[at, :].astype(F32) + dot(att[at, :], wo[...])
-        settled = norm(mixed, ga[...]).astype(BF)
-        total = settled.astype(F32)
-        for f in range(0, 4 * D, D):
-            hidden = jnp.maximum(dot(settled, wu[:, f : f + D]), 0.0).astype(BF)
-            total = total + dot(hidden, wd[f : f + D, :])
+        settled.append(norm(mixed, ga[...]).astype(BF))
+    for i, at in enumerate(chunks):
+        hidden = jnp.maximum(dot(settled[i], wu[...]), 0.0).astype(BF)
+        total = settled[i].astype(F32) + dot(hidden, wd[...])
         outs[at, :] = norm(total, gf[...]).astype(BF)
-        pltpu.make_async_copy(outs.at[at], out_hbm.at[at], out_sem.at[r // BLK]).start()
 
     wait_bytes(r3.at[pl.ds(0, 7)], s4r)
     vout[...] = r3[...].reshape(VN, D).astype(BF)
-    last = pltpu.make_async_copy(vout, vout_hbm, out_sem.at[2])
-    last.start()
 
     to_up.wait_send()
     to_down.wait_send()
@@ -385,18 +415,14 @@
 
     @pl.when(d < 8)
     def _():
+        wait_bytes(c1, s2s)
+
+    @pl.when(d >= 8)
+    def _():
         wait_bytes(c1.at[pl.ds(0, 7)], s2s)
         wait_bytes(r2.at[pl.ds(0, 15), :, pl.ds(0, D)], s3s)
 
-    @pl.when(d >= 8)
-    def _():
-        wait_bytes(c1, s2s)
-
     wait_bytes(r3.at[pl.ds(0, 7)], s4s)
-    for r in range(0, N, BLK):
-        at = pl.ds(r, BLK)
-        pltpu.make_async_copy(outs.at[at], out_hbm.at[at], out_sem.at[r // BLK]).wait()
-    last.wait()
 
 
 def vx32_row(vx, v):
@@ -433,23 +459,20 @@
         vmem((CAP, 128), jnp.int32), vmem((4, N), jnp.int32), vmem((1, N), jnp.int32),
         vmem((128 * CAP, D), BF), vmem((D, D), BF), vmem((H, N, 128), BF), vmem((ROWS, N), F32),
         vmem((BLK, D), BF), vmem((H, VR, BLK), BF), vmem((H, N), F32),
-        vmem((H, AR, N), F32), vmem((D, N), BF), vmem((N, D), BF),
+        vmem((H, AR, N), F32), vmem((D, N), BF),
         vmem((VN, D), F32), vmem((VN, D), F32), vmem((VN, D), F32), vmem((VN, D), BF),
         vmem((VN, N), F32), vmem((VN, PART), F32), vmem((8, 8, PART), F32),
         vmem((8, 1, PART), F32), vmem((16, 1, PART), F32), vmem((8, 1, D), F32),
-        vmem((8, 8, D), F32), vmem((1, 1, D), F32), vmem((VN, D), BF),
-        dma((15,)), dma((3,)), dma, dma((GROUPS,)), dma((2,)), dma((2,)),
+        vmem((8, 8, D), F32), vmem((1, 1, D), F32),
+        dma((15,)), dma, dma((GROUPS,)), dma((2,)), dma((2,)),
         dma, dma, dma, dma, dma, dma, dma, dma,
     ]
     hbm = pl.BlockSpec(memory_space=pl.ANY)
     node, virtual = pl.pallas_call(
         kernel,
-        out_shape=(
-            jax.ShapeDtypeStruct((N, D), BF),
-            jax.ShapeDtypeStruct((VN, D), BF),
-        ),
+        out_shape=(vmem((N, D), BF), vmem((VN, D), BF)),
         in_specs=[hbm] * len(args),
-        out_specs=(hbm, hbm),
+        out_specs=(pl.BlockSpec(memory_space=vmem),) * 2,
         scratch_shapes=scratch,
         compiler_params=pltpu.CompilerParams(
             collective_id=0, has_side_effects=True, vmem_limit_bytes=56 * 1024 * 1024
@@ -461,10 +484,10 @@
             jax.ShapeDtypeStruct((N, D), BF),
             jax.ShapeDtypeStruct((VN, D), BF),
         ),
-        in_specs=[hbm] * 2,
+        in_specs=[pl.BlockSpec(memory_space=vmem)] * 2,
         out_specs=(hbm, hbm),
         scratch_shapes=[dma((5,))],
-        compiler_params=pltpu.CompilerParams(vmem_limit_bytes=60 * 1024 * 1024),
+        compiler_params=pltpu.CompilerParams(vmem_limit_bytes=16 * 1024 * 1024),
     )(node, virtual)
 
 

time: 79.8 us -> 50.1 us (0.63)
  Pallas kernels: 79.1 us -> 49.3 us
    pallas_call x1, Pallas kernels: 19 us -> 0.85 us  [shards(): pl.pallas_call(hand_over, out_shape=(jax.ShapeDtypeStruct((N, D), BF), ja...]
    pallas_call x1, Pallas kernels: 60 us -> 48.5 us  [shards(): pl.pallas_call(kernel, out_shape=(vmem((N, D), BF), vmem((VN, D), BF)), i...]
where the time goes in v5:
time: 50.1 us; the launch traced here: 50 us
  Pallas kernels  49.3 us (98%)
  between operations  0.64 us (1%)
    pallas_call x1, Pallas kernels, shards(): pl.pallas_call(kernel, out_shape=(vmem((N, D), BF), vmem((VN, D), BF)), i...  48.5 us

profile of v5, /device:TPU:1, one launch (start us, length us, event | category | flops | bytes accessed | tf_op | source)
XLA Modules:
  0.0 50.0 jit_solution(16384610851611322507)
XLA Ops:
  0.6 48.5 %shard_map.158 = (bf16[512,512]{1,0:T(8,128)(2,1)S(1)}, bf16[64,512]{1,0:T(8,128)(2,1)S(1)}) custom-call(bf16[512,512]{1,0:T(8,128)(2,1)} %x_hbm.1, bf16[64,512]{1,0:T(8,128)(2,1)} %vx_hbm.1, bf16[512,512]{1,0:T(8,128)(2,1)} %wq_hbm.1, bf16[512,512]{1,0:T(8,128)(2,1)} %wk_hbm.1, bf16[512,512]{1,0:T(8,128)(2,1)} %wv_hbm.1, bf16[512,512]{1,0:T(8,128)(2,1)} %wo_hbm.1, ...), custom_call_target="tpu_custom_call" | custom-call | tf_op jit(solution)/shard_map/pallas_call | solution.py:471
  49.1 0.9 %shard_map.159 = (bf16[512,512]{1,0:T(8,128)(2,1)}, bf16[64,512]{1,0:T(8,128)(2,1)}) custom-call(bf16[512,512]{1,0:T(8,128)(2,1)S(1)} %get-tuple-element.4.node, bf16[64,512]{1,0:T(8,128)(2,1)S(1)} %get-tuple-element.5.virtual), custom_call_target="tpu_custom_call" | custom-call | tf_op jit(solution)/shard_map/pallas_call | solution.py:481

commit v6 on v5

--- a/solution.py
+++ b/solution.py
@@ -78,7 +78,7 @@
         (ga_hbm, ga), (gf_hbm, gf), (wo_hbm, wo), (wu_hbm, wu), (wd_hbm, wd),
     ]
     loads = [pltpu.make_async_copy(a, b, in_sem.at[i]) for i, (a, b) in enumerate(order)]
-    for load in loads:
+    for load in loads[:2]:
         load.start()
 
     barrier = pltpu.get_barrier_semaphore()
@@ -95,6 +95,9 @@
         return carry
 
     lax.fori_loop(1, 16, greet_dom, 0)
+
+    for load in loads[2:]:
+        load.start()
 
     loads[0].wait()
     loads[1].wait()
@@ -138,7 +141,7 @@
                     ssem, rsem.at[group], device_id=(tg, td), device_id_type=MESH,
                 ).start()
 
-    late = jnp.minimum(x, 2) + jnp.minimum(y, 2) + z >= 5
+    late = jnp.minimum(x, 2) + jnp.minimum(y, 2) + z >= 6
 
     def begin():
         to_up.start()
@@ -303,7 +306,7 @@
             def _():
                 r2[d] = c1[d - 8]
 
-        @pl.when((b == FIRST_EXP + 6) & (d >= 8))
+        @pl.when((b == FIRST_EXP + 5) & (d >= 8))
         def _():
             wait_bytes(r2.at[pl.ds(0, 15)], s2r)
             mixed, top, total = combine([r2[i] for i in range(16)])

time: 50.1 us -> 49.9 us (level)
  no operation moved by 1% of the time
where the time goes in v6:
time: 49.9 us; the launch traced here: 49.8 us
  Pallas kernels  49.2 us (99%)
  between operations  0.64 us (1%)
    pallas_call x1, Pallas kernels, shards(): pl.pallas_call(kernel, out_shape=(vmem((N, D), BF), vmem((VN, D), BF)), i...  48.3 us

profile of v6, /device:TPU:1, one launch (start us, length us, event | category | flops | bytes accessed | tf_op | source)
XLA Modules:
  0.0 49.8 jit_solution(8549139075988762009)
XLA Ops:
  0.6 48.3 %shard_map.158 = (bf16[512,512]{1,0:T(8,128)(2,1)S(1)}, bf16[64,512]{1,0:T(8,128)(2,1)S(1)}) custom-call(bf16[512,512]{1,0:T(8,128)(2,1)} %x_hbm.1, bf16[64,512]{1,0:T(8,128)(2,1)} %vx_hbm.1, bf16[512,512]{1,0:T(8,128)(2,1)} %wq_hbm.1, bf16[512,512]{1,0:T(8,128)(2,1)} %wk_hbm.1, bf16[512,512]{1,0:T(8,128)(2,1)} %wv_hbm.1, bf16[512,512]{1,0:T(8,128)(2,1)} %wo_hbm.1, ...), custom_call_target="tpu_custom_call" | custom-call | tf_op jit(solution)/shard_map/pallas_call | solution.py:474
  49.0 0.9 %shard_map.159 = (bf16[512,512]{1,0:T(8,128)(2,1)}, bf16[64,512]{1,0:T(8,128)(2,1)}) custom-call(bf16[512,512]{1,0:T(8,128)(2,1)S(1)} %get-tuple-element.4.node, bf16[64,512]{1,0:T(8,128)(2,1)S(1)} %get-tuple-element.5.virtual), custom_call_target="tpu_custom_call" | custom-call | tf_op jit(solution)/shard_map/pallas_call | solution.py:484
